TPU v7x, 128 devices: a whole 4x4x4 slice. The times are simulated.
128 devices in a mesh: row: 16 (over x, z), col: 8 (over y, core).
Axes of the slice: x: 4, y: 4, z: 4, core: 2. Of those that a mesh axis runs over, the one named last changes fastest.
Arguments:
- weight: bfloat16 [16384, 39936], P('row', 'col'), may hold values from -8 to 8
- sketch: bfloat16 [39936, 128], P('col'), may hold values from -6 to 6
Outputs:
- factor_a: float32 [16384, 128], P('row')
- factor_b: float32 [128, 39936], P(None, 'col')
- residual: bfloat16 [16384, 39936], P('row', 'col')
All inputs are finite; a program needn't handle non-finite values.
Results may differ from a plain program's by a relative error of at most 0.0029.
Values may be sent and summed in bfloat16 or wider, within the bound.
A program may use at most 128 MiB of HBM per device.

v0:
```python
import jax
import jax.numpy as jnp
from jax import lax
from jax.sharding import PartitionSpec as P

POWER = 2
NS_ITERS = 12


HIGH = lax.Precision.HIGHEST


def orthonormal(panel, reduce_gram):
    for turn in range(2):
        gram = reduce_gram(
            jnp.dot(panel.T, panel, precision=HIGH, preferred_element_type=jnp.float32)
        )
        lower = jnp.linalg.cholesky(gram)
        panel = jax.scipy.linalg.solve_triangular(lower, panel.T, lower=True).T
    return panel


def sqrt_pair(matrix):
    scale = jnp.sqrt(jnp.sum(matrix * matrix))
    eye = jnp.eye(matrix.shape[0], dtype=jnp.float32)
    upper = matrix / scale
    inverse = eye
    for turn in range(NS_ITERS):
        middle = 1.5 * eye - 0.5 * jnp.dot(inverse, upper, precision=HIGH)
        upper = jnp.dot(upper, middle, precision=HIGH)
        inverse = jnp.dot(middle, inverse, precision=HIGH)
    return (upper * jnp.sqrt(scale), inverse / jnp.sqrt(scale))


def transposed(weight, basis):
    return lax.dot_general(
        weight, basis, (((0,), (0,)), ((), ())), preferred_element_type=jnp.float32
    )


def gram_over_rows(gram):
    return lax.psum(gram, "row")


def gram_over_cols(gram):
    return lax.psum(gram, "col")


def on_device(weight, sketch):
    factor = sketch
    for step in range(POWER + 1):
        tall = lax.psum(jnp.dot(weight, factor, preferred_element_type=jnp.float32), "col")
        basis = orthonormal(tall, gram_over_rows)
        wide = lax.psum(transposed(weight, basis.astype(jnp.bfloat16)), "row")
        if step < POWER:
            factor = orthonormal(wide, gram_over_cols).astype(jnp.bfloat16)
    gram = gram_over_cols(jnp.dot(wide.T, wide, precision=HIGH, preferred_element_type=jnp.float32))
    half, inv_half = sqrt_pair(gram)
    quarter, inv_quarter = sqrt_pair(half)
    factor_a = jnp.dot(basis, quarter, precision=HIGH)
    factor_b = jnp.dot(inv_quarter, wide.T, precision=HIGH)
    residual = (weight.astype(jnp.float32) - jnp.dot(factor_a, factor_b, precision=HIGH)).astype(
        jnp.bfloat16
    )
    return (factor_a, factor_b, residual)


def solution(mesh):
    return jax.shard_map(
        on_device,
        mesh=mesh,
        in_specs=(P("row", "col"), P("col", None)),
        out_specs=(P("row", None), P(None, "col"), P("row", "col")),
        check_vma=False,
    )
```

profile of v0, /device:TPU:1, one launch (start us, length us, event | category | flops | bytes accessed | tf_op | source)
XLA Modules:
  0.0 1647.6 jit_solution(17408635366229879811)
XLA Ops:
  16.0 62.0 %all-reduce.18.cloned.1.call-done = f32[1024,128]{1,0:T(8,128)} async-done(((f32[1024,128]{1,0:T(8,128)}), f32[1024,128]{1,0:T(8,128)}) %all-reduce.18.cloned.1.call-update) | async-done | bytes 524304 | tf_op jit(solution)/shard_map/psum | solution.py:52
  81.0 81.8 %all-reduce.20.cloned.1.call-done = f32[128,128]{0,1:T(8,128)} async-done(((f32[128,128]{0,1:T(8,128)}), f32[128,128]{0,1:T(8,128)}) %all-reduce.20.cloned.1.call-update) | async-done | bytes 65552 | tf_op jit(solution)/shard_map/psum | solution.py:42
  164.6 11.7 cholesky.164
  190.7 80.1 %all-reduce.22.cloned.1.call-done = f32[128,128]{0,1:T(8,128)} async-done(((f32[128,128]{0,1:T(8,128)}), f32[128,128]{0,1:T(8,128)}) %all-reduce.22.cloned.1.call-update) | async-done | bytes 65552 | tf_op jit(solution)/shard_map/psum | solution.py:42
  272.6 11.7 cholesky.175
  303.1 92.9 %all-reduce.24.cloned.1.call-done = f32[4992,128]{0,1:T(8,128)} async-done(((f32[4992,128]{0,1:T(8,128)}), f32[4992,128]{0,1:T(8,128)}) %all-reduce.24.cloned.1.call-update) | async-done | bytes 2555920 | tf_op jit(solution)/shard_map/psum | solution.py:54
  402.1 56.5 %all-reduce.26.cloned.1.call-done = f32[128,128]{0,1:T(8,128)} async-done(((f32[128,128]{0,1:T(8,128)}), f32[128,128]{0,1:T(8,128)}) %all-reduce.26.cloned.1.call-update) | async-done | bytes 65552 | tf_op jit(solution)/shard_map/psum | solution.py:46
  460.5 11.7 cholesky.186
  492.3 57.7 %all-reduce.28.cloned.1.call-done = f32[128,128]{0,1:T(8,128)} async-done(((f32[128,128]{0,1:T(8,128)}), f32[128,128]{0,1:T(8,128)}) %all-reduce.28.cloned.1.call-update) | async-done | bytes 65552 | tf_op jit(solution)/shard_map/psum | solution.py:46
  551.8 11.7 cholesky.197
  586.9 59.9 %all-reduce.30.cloned.1.call-done = f32[1024,128]{0,1:T(8,128)} async-done(((f32[1024,128]{0,1:T(8,128)}), f32[1024,128]{0,1:T(8,128)}) %all-reduce.30.cloned.1.call-update) | async-done | bytes 524304 | tf_op jit(solution)/shard_map/psum | solution.py:52
  649.5 81.7 %all-reduce.32.cloned.1.call-done = f32[128,128]{0,1:T(8,128)} async-done(((f32[128,128]{0,1:T(8,128)}), f32[128,128]{0,1:T(8,128)}) %all-reduce.32.cloned.1.call-update) | async-done | bytes 65552 | tf_op jit(solution)/shard_map/psum | solution.py:42
  733.0 11.7 cholesky.208
  759.3 79.9 %all-reduce.34.cloned.1.call-done = f32[128,128]{0,1:T(8,128)} async-done(((f32[128,128]{0,1:T(8,128)}), f32[128,128]{0,1:T(8,128)}) %all-reduce.34.cloned.1.call-update) | async-done | bytes 65552 | tf_op jit(solution)/shard_map/psum | solution.py:42
  841.0 11.7 cholesky.219
  871.5 92.8 %all-reduce.36.cloned.1.call-done = f32[4992,128]{0,1:T(8,128)} async-done(((f32[4992,128]{0,1:T(8,128)}), f32[4992,128]{0,1:T(8,128)}) %all-reduce.36.cloned.1.call-update) | async-done | bytes 2555920 | tf_op jit(solution)/shard_map/psum | solution.py:54
  970.2 56.7 %all-reduce.38.cloned.1.call-done = f32[128,128]{0,1:T(8,128)} async-done(((f32[128,128]{0,1:T(8,128)}), f32[128,128]{0,1:T(8,128)}) %all-reduce.38.cloned.1.call-update) | async-done | bytes 65552 | tf_op jit(solution)/shard_map/psum | solution.py:46
  1060.6 57.7 %all-reduce.40.cloned.1.call-done = f32[128,128]{0,1:T(8,128)} async-done(((f32[128,128]{0,1:T(8,128)}), f32[128,128]{0,1:T(8,128)}) %all-reduce.40.cloned.1.call-update) | async-done | bytes 65552 | tf_op jit(solution)/shard_map/psum | solution.py:46
  1155.2 59.9 %all-reduce.42.cloned.1.call-done = f32[1024,128]{0,1:T(8,128)} async-done(((f32[1024,128]{0,1:T(8,128)}), f32[1024,128]{0,1:T(8,128)}) %all-reduce.42.cloned.1.call-update) | async-done | bytes 524304 | tf_op jit(solution)/shard_map/psum | solution.py:52
  1217.9 81.7 %all-reduce.44.cloned.1.call-done = f32[128,128]{0,1:T(8,128)} async-done(((f32[128,128]{0,1:T(8,128)}), f32[128,128]{0,1:T(8,128)}) %all-reduce.44.cloned.1.call-update) | async-done | bytes 65552 | tf_op jit(solution)/shard_map/psum | solution.py:42
  1327.4 80.1 %all-reduce.46.cloned.1.call-done = f32[128,128]{0,1:T(8,128)} async-done(((f32[128,128]{0,1:T(8,128)}), f32[128,128]{0,1:T(8,128)}) %all-reduce.46.cloned.1.call-update) | async-done | bytes 65552 | tf_op jit(solution)/shard_map/psum | solution.py:42
  1440.1 92.7 %all-reduce.48.cloned.1.call-done = f32[4992,128]{0,1:T(8,128)} async-done(((f32[4992,128]{0,1:T(8,128)}), f32[4992,128]{0,1:T(8,128)}) %all-reduce.48.cloned.1.call-update) | async-done | bytes 2555920 | tf_op jit(solution)/shard_map/psum | solution.py:54
  1538.4 57.0 %all-reduce.50.cloned.1.call-done = f32[128,128]{1,0:T(8,128)} async-done(((f32[128,128]{1,0:T(8,128)}), f32[128,128]{1,0:T(8,128)}) %all-reduce.50.cloned.1.call-update) | async-done | bytes 65552 | tf_op jit(solution)/shard_map/psum | solution.py:46
  1619.2 21.5 %subtract_convert_fusion = bf16[1024,4992]{1,0:T(8,128)(2,1)} fusion(bf16[1024,4992]{1,0:T(8,128)(2,1)} %param.7, f32[1024,128]{1,0:T(8,128)S(1)} %fusion.140, f32[128,4992]{1,0:T(8,128)S(1)} %fusion.141), kind=kOutput, calls=%fused_computation | convolution fusion | flops 7867072512 | bytes 23527424 | tf_op jit(solution)/shard_map/dot_general | solution.py:62
  (211 shorter events, 307.9 us)
Async XLA Ops:
  7.2 1.3 copy-start
  7.2 70.9 %all-reduce.18.cloned.1.call-start = ((), (), s32[]{:S(2)}) async-start(), calls=%async_computation | async-start | bytes 1048576 | tf_op jit(solution)/shard_map/psum | solution.py:52
  16.0 146.8 %all-reduce.20.cloned.1.call-start = ((), (), s32[]{:S(2)}) async-start(), calls=%async_computation.1 | async-start | bytes 131072 | tf_op jit(solution)/shard_map/psum | solution.py:42
  80.9 189.8 %all-reduce.22.cloned.1.call-start = ((), (), s32[]{:S(2)}) async-start(), calls=%async_computation.2 | async-start | bytes 131072 | tf_op jit(solution)/shard_map/psum | solution.py:42
  190.4 205.6 %all-reduce.24.cloned.1.call-start = ((), (), s32[]{:S(2)}) async-start(), calls=%async_computation.3 | async-start | bytes 5111808 | tf_op jit(solution)/shard_map/psum | solution.py:54
  303.0 155.6 %all-reduce.26.cloned.1.call-start = ((), (), s32[]{:S(2)}) async-start(), calls=%async_computation.4 | async-start | bytes 131072 | tf_op jit(solution)/shard_map/psum | solution.py:46
  401.7 148.3 %all-reduce.28.cloned.1.call-start = ((), (), s32[]{:S(2)}) async-start(), calls=%async_computation.5 | async-start | bytes 131072 | tf_op jit(solution)/shard_map/psum | solution.py:46
  487.4 1.5 copy-start.1
  492.1 154.7 %all-reduce.30.cloned.1.call-start = ((), (), s32[]{:S(2)}) async-start(), calls=%async_computation.6 | async-start | bytes 1048576 | tf_op jit(solution)/shard_map/psum | solution.py:52
  586.9 144.4 %all-reduce.32.cloned.1.call-start = ((), (), s32[]{:S(2)}) async-start(), calls=%async_computation.7 | async-start | bytes 131072 | tf_op jit(solution)/shard_map/psum | solution.py:42
  649.3 189.9 %all-reduce.34.cloned.1.call-start = ((), (), s32[]{:S(2)}) async-start(), calls=%async_computation.8 | async-start | bytes 131072 | tf_op jit(solution)/shard_map/psum | solution.py:42
  758.8 205.4 %all-reduce.36.cloned.1.call-start = ((), (), s32[]{:S(2)}) async-start(), calls=%async_computation.9 | async-start | bytes 5111808 | tf_op jit(solution)/shard_map/psum | solution.py:54
  871.4 155.5 %all-reduce.38.cloned.1.call-start = ((), (), s32[]{:S(2)}) async-start(), calls=%async_computation.10 | async-start | bytes 131072 | tf_op jit(solution)/shard_map/psum | solution.py:46
  970.0 148.3 %all-reduce.40.cloned.1.call-start = ((), (), s32[]{:S(2)}) async-start(), calls=%async_computation.11 | async-start | bytes 131072 | tf_op jit(solution)/shard_map/psum | solution.py:46
  1055.6 1.5 copy-start.2
  1060.3 154.7 %all-reduce.42.cloned.1.call-start = ((), (), s32[]{:S(2)}) async-start(), calls=%async_computation.12 | async-start | bytes 1048576 | tf_op jit(solution)/shard_map/psum | solution.py:52
  1155.1 144.5 %all-reduce.44.cloned.1.call-start = ((), (), s32[]{:S(2)}) async-start(), calls=%async_computation.13 | async-start | bytes 131072 | tf_op jit(solution)/shard_map/psum | solution.py:42
  1217.5 190.1 %all-reduce.46.cloned.1.call-start = ((), (), s32[]{:S(2)}) async-start(), calls=%async_computation.14 | async-start | bytes 131072 | tf_op jit(solution)/shard_map/psum | solution.py:42
  1327.2 205.5 %all-reduce.48.cloned.1.call-start = ((), (), s32[]{:S(2)}) async-start(), calls=%async_computation.15 | async-start | bytes 5111808 | tf_op jit(solution)/shard_map/psum | solution.py:54
  1439.8 155.5 %all-reduce.50.cloned.1.call-start = ((), (), s32[]{:S(2)}) async-start(), calls=%async_computation.16 | async-start | bytes 131072 | tf_op jit(solution)/shard_map/psum | solution.py:46
  1611.3 5.2 copy-start.3
  1616.5 2.6 copy-start.5
  1619.2 21.5 %copy-start.4 = (f32[128,4992]{1,0:T(8,128)}, f32[128,4992]{1,0:T(8,128)S(1)}, u32[]{:S(2)}) copy-start(f32[128,4992]{1,0:T(8,128)S(1)} %fusion.141) | copy-start | bytes 7667716
Sparse Core Ops, SparseCore 0:
  16.1 61.9 all-reduce.17
  82.2 80.5 all-reduce.19
  190.5 80.2 all-reduce.21
  303.1 92.7 all-reduce.23
  401.8 56.8 all-reduce.25
  492.2 57.7 all-reduce.27
  587.0 59.7 all-reduce.29
  650.6 80.5 all-reduce.31
  758.9 80.1 all-reduce.33
  871.5 92.6 all-reduce.35
  970.1 56.7 all-reduce.37
  1060.5 57.7 all-reduce.39
  1155.2 59.7 all-reduce.41
  1219.0 80.5 all-reduce.43
  1327.3 80.2 all-reduce.45
  1439.9 92.7 all-reduce.47
  1538.5 56.8 all-reduce.49
where the time goes:
time: 1660 us; the launch traced here: 1650 us
  waiting for transfers between devices  1230 us (74%)
  other arithmetic  239 us (14%)
  matrix products  144 us (9%)
  between operations  16.9 us (1%)
    psum x6, waiting for transfers between devices, gram_over_rows(): return lax.psum(gram, 'row')  485 us
    psum x5, waiting for transfers between devices, gram_over_cols(): return lax.psum(gram, 'col')  286 us
    psum x3, waiting for transfers between devices, on_device(): wide = lax.psum(transposed(weight, basis.astype(jnp.bfloat16)), 'row')  278 us
    psum x3, waiting for transfers between devices, on_device(): lax.psum(jnp.dot(weight, factor, preferred_element_type=jnp.float32), 'col')  182 us
    another operation x30, other arithmetic, orthonormal(): lower = jnp.linalg.cholesky(gram)  124 us
    another operation x20, other arithmetic, orthonormal(): panel = jax.scipy.linalg.solve_triangular(lower, panel.T, lower=True).T  105 us
  transfers between devices with their start and end apart: 17, of which 17 were waited for; matrix products, arithmetic and copies ran while one was open for 0% of the time, Pallas kernels for 0%

commit v1 on v0

v1 whole, which is shorter than its diff:
```python
import jax
import jax.numpy as jnp
from jax import lax
from jax.experimental import pallas as pl
from jax.experimental.pallas import tpu as pltpu
from jax.sharding import PartitionSpec as P

POWER = 2
NS_ITERS = 12
RANK = 128
ROWS = 1024
COLS = 4992
PAD = 5120
NCOL = 8
NROW = 16
PART = PAD // 4
OWN = PAD // NROW
PIECE = PART // NROW
TALL = ROWS // NCOL
SEG = RANK // NCOL
STEPS = POWER + 1
TILE = 384

f32 = jnp.float32
bf16 = jnp.bfloat16
MESH = pl.DeviceIdType.MESH

ORDER = ((0, 2, 1, 3), (2, 1, 3, 0), (1, 3, 0, 2), (3, 0, 2, 1))


def split3(a):
    hi = a.astype(bf16)
    rest = a - hi.astype(f32)
    mid = rest.astype(bf16)
    low = (rest - mid.astype(f32)).astype(bf16)
    return hi, mid, low


def left6(a, axis):
    hi, mid, low = split3(a)
    return jnp.concatenate([hi, hi, mid, hi, low, mid], axis)


def right6(a, axis):
    hi, mid, low = split3(a)
    return jnp.concatenate([hi, mid, hi, low, hi, mid], axis)


def mm(a, b):
    return jnp.dot(left6(a, 1), right6(b, 0), preferred_element_type=f32)


def gram_of(y):
    return lax.dot_general(
        left6(y, 0), right6(y, 0), (((0,), (0,)), ((), ())), preferred_element_type=f32
    )


def eye_of():
    r = lax.broadcasted_iota(jnp.int32, (RANK, RANK), 0)
    c = lax.broadcasted_iota(jnp.int32, (RANK, RANK), 1)
    return jnp.where(r == c, 1.0, 0.0).astype(f32)


def cholesky_inverse(gram, s_ref, m_ref, hook):
    s_ref[:, 0:RANK] = gram
    s_ref[:, RANK:] = eye_of()
    sub = lax.broadcasted_iota(jnp.int32, (8, RANK), 0)
    lane = lax.broadcasted_iota(jnp.int32, (8, RANK), 1)
    for k in range(RANK // 8):
        o = 8 * k
        hook(k)
        a_rows = s_ref[o : o + 8, 0:RANK]
        n_rows = s_ref[o : o + 8, RANK:]
        d = [[None] * 8 for _ in range(8)]
        l = [[None] * 8 for _ in range(8)]
        inv = [None] * 8
        for j in range(8):
            column = jnp.broadcast_to(a_rows[:, o + j : o + j + 1], (8, RANK))
            for i in range(j, 8):
                d[i][j] = jnp.broadcast_to(column[i : i + 1, :], (8, RANK))
        for j in range(8):
            inv[j] = lax.rsqrt(d[j][j])
            for i in range(j + 1, 8):
                l[i][j] = d[i][j] * inv[j]
            for i in range(j + 1, 8):
                for c in range(j + 1, i + 1):
                    d[i][c] = d[i][c] - l[i][j] * l[c][j]
        ua = [None] * 8
        un = [None] * 8
        u = jnp.zeros((8, RANK), f32)
        n = jnp.zeros((8, RANK), f32)
        for i in range(8):
            a = jnp.broadcast_to(a_rows[i : i + 1, :], (8, RANK))
            b = jnp.broadcast_to(n_rows[i : i + 1, :], (8, RANK))
            for c in range(i):
                a = a - l[i][c] * ua[c]
                b = b - l[i][c] * un[c]
            ua[i] = a * inv[i]
            un[i] = b * inv[i]
            u = jnp.where(sub == i, ua[i], u)
            n = jnp.where(sub == i, un[i], n)
        m_ref[o : o + 8, :] = n
        if o + 8 < RANK:
            u = jnp.where(lane >= o + 8, u, 0.0)
            parts = []
            for v in (u, n):
                hi = v.astype(bf16).astype(f32)
                mid = (v - hi).astype(bf16).astype(f32)
                parts.append((hi, mid, v - hi - mid))
            (uh, um, ul), (nh, nm, nl) = parts
            left = jnp.concatenate([uh, uh, um, uh, ul, um], 0)
            right = jnp.concatenate(
                [
                    jnp.concatenate([uh, um, uh, ul, uh, um], 0),
                    jnp.concatenate([nh, nm, nh, nl, nh, nm], 0),
                ],
                1,
            )
            change = lax.dot_general(
                left, right, (((0,), (0,)), ((), ())), preferred_element_type=f32
            )
            s_ref[o + 8 :, :] = s_ref[o + 8 :, :] - change[o + 8 :, :]


def factors_kernel(
    w_hbm, sketch_ref, basis_ref, wide_ref, q_ref, iq_ref,
    w_ref, fac, b16, part, tall_in, tall_all, rb0, rb1, rb2, rb3, wide_all,
    own, g_ref, ar1, ar2, ar3, s_ref, m_ref, total_ref, y_ref,
    w_sem, ar_send, ar_recv, t_send, t_recv, ta_send, ta_recv, r_send, r_recv, a_send, a_recv,
):
    row = lax.axis_index("row")
    col = lax.axis_index("col")
    y = col // 2
    x = row // 4
    z = row % 4
    partner = ((x + 1 - 2 * (x % 2)) * 4 + z, (3 - x) * 4 + z, x * 4 + z + 1 - 2 * (z % 2), x * 4 + 3 - z)
    xhi, zhi = x // 2, z // 2
    bit = ((x + xhi) % 2, xhi, (z + zhi) % 2, zhi)

    w_copy = pltpu.make_async_copy(w_hbm, w_ref.at[:, pl.ds(0, COLS)], w_sem)
    w_copy.start()

    barrier = pltpu.get_barrier_semaphore()
    for d in range(1, NCOL):
        pl.semaphore_signal(barrier, inc=1, device_id={"col": (col + d) % NCOL}, device_id_type=MESH)
    for d in range(1, NROW):
        pl.semaphore_signal(barrier, inc=1, device_id={"row": (row + d) % NROW}, device_id_type=MESH)

    w_ref[:, pl.ds(COLS, PAD - COLS)] = jnp.zeros((ROWS, PAD - COLS), bf16)
    fac[pl.ds(0, COLS), :] = sketch_ref[...]
    fac[pl.ds(COLS, PAD - COLS), :] = jnp.zeros((PAD - COLS, RANK), bf16)
    pl.semaphore_wait(barrier, NCOL + NROW - 2)
    w_copy.wait()

    def send(src, dst, send_sem, recv_sem, to):
        pltpu.make_async_remote_copy(
            src_ref=src, dst_ref=dst, send_sem=send_sem, recv_sem=recv_sem, device_id=to, device_id_type=MESH
        ).start()

    def wait(ref, sem):
        pltpu.make_async_copy(ref, ref, sem).wait()

    def all_reduce(index):
        first, second, third = ar1.at[index], ar2.at[index], ar3.at[index]
        for d in range(1, NCOL):
            peer = (col + d) % NCOL
            send(g_ref.at[pl.ds(pl.multiple_of(peer * SEG, SEG), SEG), :], first.at[col],
                 ar_send.at[index, 0], ar_recv.at[index, 0], {"col": peer})
        mine = pl.ds(pl.multiple_of(col * SEG, SEG), SEG)
        first[col] = g_ref[mine, :]
        wait(first.at[pl.ds(0, NCOL - 1)], ar_recv.at[index, 0])
        second[row] = jnp.sum(first[...], axis=0)
        for d in range(1, NROW):
            send(second.at[row], second.at[row], ar_send.at[index, 1], ar_recv.at[index, 1],
                 {"row": (row + d) % NROW})
        wait(second.at[pl.ds(0, NROW - 1)], ar_recv.at[index, 1])
        third[mine, :] = jnp.sum(second[...], axis=0)
        for d in range(1, NCOL):
            send(third.at[mine, :], third.at[mine, :], ar_send.at[index, 2], ar_recv.at[index, 2],
                 {"col": (col + d) % NCOL})
        wait(third.at[pl.ds(0, SEG * (NCOL - 1)), :], ar_recv.at[index, 2])
        wait(first.at[pl.ds(0, NCOL - 1)], ar_send.at[index, 0])
        wait(second.at[pl.ds(0, NROW - 1)], ar_send.at[index, 1])
        wait(third.at[pl.ds(0, SEG * (NCOL - 1)), :], ar_send.at[index, 2])

    def orth(rows, base, hook):
        def one(turn, carry):
            panel = own[pl.ds(0, rows), :]
            g_ref[...] = gram_of(panel)
            all_reduce(base + turn)
            cholesky_inverse(ar3[base + turn], s_ref, m_ref, lambda k: hook(turn, k))
            inverse = m_ref[...]

            @pl.when(turn == 0)
            def _():
                total_ref[...] = inverse.T
                own[pl.ds(0, rows), :] = mm(own[pl.ds(0, rows), :], inverse.T)

            @pl.when(turn == 1)
            def _():
                total_ref[...] = mm(total_ref[...], inverse.T)

            return carry

        lax.fori_loop(0, 2, one, 0)

    def step(k, carry):
        mine = pl.ds(pl.multiple_of(col * TALL, TALL), TALL)
        tall_k = tall_in.at[k]

        def tall_pair(j, carry):
            pair = (y + 1 + j) % 4
            at = pl.ds(pl.multiple_of(pair * 2 * TALL, 2 * TALL), 2 * TALL)
            y_ref[at, :] = jnp.dot(w_ref[at, :], fac[...], preferred_element_type=f32)

            @pl.when(j < 3)
            def _():
                for core in range(2):
                    peer = pair * 2 + core
                    send(y_ref.at[pl.ds(pl.multiple_of(peer * TALL, TALL), TALL), :], tall_k.at[col],
                         t_send.at[k], t_recv.at[k], {"col": peer})

            return carry

        lax.fori_loop(0, 4, tall_pair, 0)
        peer = col + 1 - 2 * (col % 2)
        send(y_ref.at[pl.ds(pl.multiple_of(peer * TALL, TALL), TALL), :], tall_k.at[col],
             t_send.at[k], t_recv.at[k], {"col": peer})
        tall_k[col] = y_ref[mine, :]
        wait(tall_k.at[pl.ds(0, NCOL - 1)], t_recv.at[k])
        wait(tall_k.at[pl.ds(0, NCOL - 1)], t_send.at[k])
        panel = jnp.sum(tall_k[...], axis=0)
        own[pl.ds(0, TALL), :] = panel
        whole = tall_all.at[k]
        whole[mine, :] = panel

        def tall_hook(turn, block):
            if block == 0:

                @pl.when(turn == 0)
                def _():
                    for d in range(1, NCOL):
                        send(whole.at[mine, :], whole.at[mine, :], ta_send.at[k], ta_recv.at[k],
                             {"col": (col + d) % NCOL})

        orth(TALL, k * 4, tall_hook)
        wait(whole.at[pl.ds(0, TALL * (NCOL - 1)), :], ta_recv.at[k])
        wait(whole.at[pl.ds(0, TALL * (NCOL - 1)), :], ta_send.at[k])

        def make_basis(t, carry):
            at = pl.ds(pl.multiple_of(t * 256, 256), 256)
            basis = mm(whole[at, :], total_ref[...])
            basis_ref[at, :] = basis
            b16[at, :] = basis.astype(bf16)
            return carry

        lax.fori_loop(0, ROWS // 256, make_basis, 0)

        buffers = (rb0.at[k], rb1.at[k], rb2.at[k], rb3.at[k])
        start = [PART * q for q in range(4)]

        def times(at):
            part[at, :] = lax.dot_general(
                w_ref[:, at], b16[...], (((0,), (0,)), ((), ())), preferred_element_type=f32
            )

        def rows_at(offset, size):
            return pl.ds(pl.multiple_of(offset, PIECE), size)

        size = PART
        for s in range(4):
            size = size // 2
            for q in range(4):
                kind = ORDER[q][s]
                at = rows_at(start[q] + (1 - bit[kind]) * size, size)
                if s == 0:
                    at = pl.ds(pl.multiple_of(start[q] + (1 - bit[kind]) * size, 128), size)
                    times(at)
                send(part.at[at, :], buffers[s].at[q], r_send.at[k, s, q], r_recv.at[k, s, q],
                     {"row": partner[kind]})
            for q in range(4):
                kind = ORDER[q][s]
                start[q] = start[q] + bit[kind] * size
                if s == 0:
                    times(pl.ds(pl.multiple_of(start[q], 128), size))
            for q in range(4):
                at = rows_at(start[q], size)
                wait(buffers[s].at[q], r_recv.at[k, s, q])
                part[at, :] = part[at, :] + buffers[s][q]
        for s in range(4):
            for q in range(4):
                wait(buffers[s].at[q], r_send.at[k, s, q])
        wide_k = wide_all.at[k]
        for q in range(4):
            at = rows_at(start[q], PIECE)
            own[pl.ds(PIECE * q, PIECE), :] = part[at, :]
            wide_k[at, :] = part[at, :]

        place = [list(start)]
        for j in range(4):
            now = list(place[-1])
            for q in range(4):
                now[q] = now[q] - bit[ORDER[q][3 - j]] * (PIECE << j)
            place.append(now)

        def gather_start(j):
            for q in range(4):
                at = rows_at(place[j][q], PIECE << j)
                send(wide_k.at[at, :], wide_k.at[at, :], a_send.at[k, j, q], a_recv.at[k, j, q],
                     {"row": partner[ORDER[q][3 - j]]})

        def gather_wait(j):
            for q in range(4):
                ref = wide_k.at[pl.ds(0, PIECE << j), :]
                wait(ref, a_recv.at[k, j, q])
                wait(ref, a_send.at[k, j, q])

        @pl.when(k < POWER)
        def _():
            def wide_hook(turn, block):
                if block in (0, 5, 10):

                    @pl.when(turn == 0)
                    def _():
                        if block:
                            gather_wait(block // 5 - 1)
                        gather_start(block // 5)

                if block == 0:

                    @pl.when(turn == 1)
                    def _():
                        gather_wait(2)
                        gather_start(3)

            orth(OWN, k * 4 + 2, wide_hook)
            gather_wait(3)

            def make_factor(t, carry):
                at = pl.ds(pl.multiple_of(t * 512, 512), 512)
                fac[at, :] = mm(wide_k[at, :], total_ref[...]).astype(bf16)
                return carry

            lax.fori_loop(0, PAD // 512, make_factor, 0)

        @pl.when(k == POWER)
        def _():
            g_ref[...] = gram_of(own[...])
            all_reduce(k * 4 + 2)
            gather_start(0)
            eye = eye_of()

            def newton(_, pair):
                upper, inverse = pair
                middle = 1.5 * eye - 0.5 * mm(inverse, upper)
                return mm(upper, middle), mm(middle, inverse)

            def sqrt_pair(matrix, hook):
                scale = jnp.sqrt(jnp.sum(matrix * matrix, keepdims=True))
                pair = (matrix / scale, eye)
                for third in range(3):
                    pair = lax.fori_loop(0, NS_ITERS // 3, newton, pair)
                    hook(third)
                root = jnp.sqrt(scale)
                return pair[0] * root, pair[1] / root

            def first(third):
                gather_wait(third)
                gather_start(third + 1)

            half, _ = sqrt_pair(ar3[k * 4 + 2], first)
            quarter, inv_quarter = sqrt_pair(half, lambda third: None)
            q_ref[...] = quarter
            iq_ref[...] = inv_quarter
            gather_wait(3)
            wide_ref[...] = wide_k[...]

        return carry

    lax.fori_loop(0, STEPS, step, 0)


def factors(weight, sketch):
    vmem = pl.BlockSpec(memory_space=pltpu.VMEM)
    dma = pltpu.SemaphoreType.DMA
    return pl.pallas_call(
        factors_kernel,
        name="factors",
        out_shape=(
            jax.ShapeDtypeStruct((ROWS, RANK), f32),
            jax.ShapeDtypeStruct((PAD, RANK), f32),
            jax.ShapeDtypeStruct((RANK, RANK), f32),
            jax.ShapeDtypeStruct((RANK, RANK), f32),
        ),
        in_specs=[pl.BlockSpec(memory_space=pl.ANY), vmem],
        out_specs=(vmem, vmem, vmem, vmem),
        scratch_shapes=[
            pltpu.VMEM((ROWS, PAD), bf16),
            pltpu.VMEM((PAD, RANK), bf16),
            pltpu.VMEM((ROWS, RANK), bf16),
            pltpu.VMEM((PAD, RANK), f32),
            pltpu.VMEM((STEPS, NCOL, TALL, RANK), f32),
            pltpu.VMEM((STEPS, ROWS, RANK), f32),
            pltpu.VMEM((STEPS, 4, PART // 2, RANK), f32),
            pltpu.VMEM((STEPS, 4, PART // 4, RANK), f32),
            pltpu.VMEM((STEPS, 4, PART // 8, RANK), f32),
            pltpu.VMEM((STEPS, 4, PART // 16, RANK), f32),
            pltpu.VMEM((STEPS, PAD, RANK), f32),
            pltpu.VMEM((OWN, RANK), f32),
            pltpu.VMEM((RANK, RANK), f32),
            pltpu.VMEM((STEPS * 4, NCOL, SEG, RANK), f32),
            pltpu.VMEM((STEPS * 4, NROW, SEG, RANK), f32),
            pltpu.VMEM((STEPS * 4, RANK, RANK), f32),
            pltpu.VMEM((RANK, 2 * RANK), f32),
            pltpu.VMEM((RANK, RANK), f32),
            pltpu.VMEM((RANK, RANK), f32),
            pltpu.VMEM((ROWS, RANK), f32),
            dma,
            dma((STEPS * 4, 3)),
            dma((STEPS * 4, 3)),
            dma((STEPS,)),
            dma((STEPS,)),
            dma((STEPS,)),
            dma((STEPS,)),
            dma((STEPS, 4, 4)),
            dma((STEPS, 4, 4)),
            dma((STEPS, 4, 4)),
            dma((STEPS, 4, 4)),
        ],
        compiler_params=pltpu.CompilerParams(
            collective_id=0, has_side_effects=True, vmem_limit_bytes=60 << 20
        ),
    )(weight, sketch)


def residual_kernel(w_ref, basis_ref, q_ref, iq_ref, wide_ref, fa_ref, fb_ref, res_ref, left):
    @pl.when(pl.program_id(0) == 0)
    def _():
        for t in range(ROWS // 256):
            at = pl.ds(t * 256, 256)
            a = mm(basis_ref[at, :], q_ref[...])
            fa_ref[at, :] = a
            hi = a.astype(bf16)
            low = (a - hi.astype(f32)).astype(bf16)
            left[at, :] = jnp.concatenate([hi, low, hi, low], 1)

    b = mm(iq_ref[...], wide_ref[...].T)
    fb_ref[...] = b
    hi = b.astype(bf16)
    low = (b - hi.astype(f32)).astype(bf16)
    product = jnp.dot(left[...], jnp.concatenate([hi, hi, low, low], 0), preferred_element_type=f32)
    res_ref[...] = (w_ref[...].astype(f32) - product).astype(bf16)


def residual(weight, basis, quarter, inv_quarter, wide):
    small = pl.BlockSpec((RANK, RANK), lambda i: (0, 0))
    panel = pl.BlockSpec((ROWS, RANK), lambda i: (0, 0))
    block = pl.BlockSpec((ROWS, TILE), lambda i: (0, i))
    return pl.pallas_call(
        residual_kernel,
        name="residual",
        grid=(COLS // TILE,),
        out_shape=(
            jax.ShapeDtypeStruct((ROWS, RANK), f32),
            jax.ShapeDtypeStruct((RANK, COLS), f32),
            jax.ShapeDtypeStruct((ROWS, COLS), bf16),
        ),
        in_specs=[block, panel, small, small, pl.BlockSpec((TILE, RANK), lambda i: (i, 0))],
        out_specs=(panel, pl.BlockSpec((RANK, TILE), lambda i: (0, i)), block),
        scratch_shapes=[pltpu.VMEM((ROWS, 4 * RANK), bf16)],
        compiler_params=pltpu.CompilerParams(vmem_limit_bytes=60 << 20),
    )(weight, basis, quarter, inv_quarter, wide)


def on_device(weight, sketch):
    basis, wide, quarter, inv_quarter = factors(weight, sketch)
    return residual(weight, basis, quarter, inv_quarter, wide)


def solution(mesh):
    return jax.shard_map(
        on_device,
        mesh=mesh,
        in_specs=(P("row", "col"), P("col", None)),
        out_specs=(P("row", None), P(None, "col"), P("row", "col")),
        check_vma=False,
    )
```

time: 1660 us -> 389 us (0.23)
  waiting for transfers between devices: 1230 us -> 0 us
  Pallas kernels: 0 us -> 386 us
  other arithmetic: 239 us -> 0 us
  matrix products: 144 us -> 0 us
    psum x17 -> x0, waiting for transfers between devices: 1230 us -> none  [the longest x6 485 us: gram_over_rows(): return lax.psum(gram, 'row')]
    pallas_call x0 -> x2, Pallas kernels: none -> 386 us  [the longest x1 367 us: factors(): pl.pallas_call(factors_kernel, name='factors', out_shape=(jax.ShapeDtypeS...]
    another operation x50 -> x0, other arithmetic: 229 us -> none  [the longest x30 124 us: orthonormal(): lower = jnp.linalg.cholesky(gram)]
    dot_general x91 -> x0, matrix products: 121 us -> none  [the longest x10 29.1 us: orthonormal(): jnp.dot(panel.T, panel, precision=HIGH, preferred_element_type=jnp.float32)]
    another operation x10 -> x0, matrix products: 23.1 us -> none  [orthonormal(): panel = jax.scipy.linalg.solve_triangular(lower, panel.T, lower=True).T]
  transfers between devices with their start and end apart: 17 -> 0, of which waited for: 17 -> 0; matrix products, arithmetic and copies ran while one was open for 0% -> 0% of each run, Pallas kernels for 0% -> 0%
where the time goes in v1:
time: 389 us; the launch traced here: 387 us
  Pallas kernels  386 us (99%)
    pallas_call x1, Pallas kernels, factors(): pl.pallas_call(factors_kernel, name='factors', out_shape=(jax.ShapeDtypeS...  367 us
    pallas_call x1, Pallas kernels, residual(): pl.pallas_call(residual_kernel, name='residual', grid=(COLS // TILE,), ou...  19.5 us

profile of v1, /device:TPU:1, one launch (start us, length us, event | category | flops | bytes accessed | tf_op | source)
XLA Modules:
  0.0 386.6 jit_solution(13885479620600751998)
XLA Ops:
  0.6 366.5 %factors.1 = (f32[1024,128]{1,0:T(8,128)}, f32[5120,128]{1,0:T(8,128)}, f32[128,128]{1,0:T(8,128)}, f32[128,128]{1,0:T(8,128)}) custom-call(bf16[1024,4992]{1,0:T(8,128)(2,1)} %w_ref.1, bf16[4992,128]{1,0:T(8,128)(2,1)} %sketch_ref.1), custom_call_target="tpu_custom_call" | custom-call | tf_op jit(solution)/shard_map/factors/pallas_call | solution.py:387
  367.2 19.5 %residual.1 = (f32[1024,128]{1,0:T(8,128)}, f32[128,4992]{1,0:T(8,128)}, bf16[1024,4992]{1,0:T(8,128)(2,1)}) custom-call(bf16[1024,4992]{1,0:T(8,128)(2,1)} %w_ref.1, f32[1024,128]{1,0:T(8,128)} %get-tuple-element.7.basis_ref, f32[128,128]{1,0:T(8,128)} %get-tuple-element.8.q_ref, f32[128,128]{1,0:T(8,128)} %get-tuple-element.9.iq_ref, ...), custom_call_target="tpu_custom_call" | custom-call | tf_op jit(solution)/shard_map/residual/pallas_call | solution.py:460

commit v2 on v1

--- a/solution.py
+++ b/solution.py
@@ -62,14 +62,13 @@
     return jnp.where(r == c, 1.0, 0.0).astype(f32)
 
 
-def cholesky_inverse(gram, s_ref, m_ref, hook):
+def cholesky_inverse(gram, s_ref, m_ref):
     s_ref[:, 0:RANK] = gram
     s_ref[:, RANK:] = eye_of()
     sub = lax.broadcasted_iota(jnp.int32, (8, RANK), 0)
     lane = lax.broadcasted_iota(jnp.int32, (8, RANK), 1)
     for k in range(RANK // 8):
         o = 8 * k
-        hook(k)
         a_rows = s_ref[o : o + 8, 0:RANK]
         n_rows = s_ref[o : o + 8, RANK:]
         d = [[None] * 8 for _ in range(8)]
@@ -126,7 +125,7 @@
 def factors_kernel(
     w_hbm, sketch_ref, basis_ref, wide_ref, q_ref, iq_ref,
     w_ref, fac, b16, part, tall_in, tall_all, rb0, rb1, rb2, rb3, wide_all,
-    own, g_ref, ar1, ar2, ar3, s_ref, m_ref, total_ref, y_ref,
+    own, g_ref, ar1, ar2, ar3, s_ref, m_ref, total_ref, second_ref, y_ref,
     w_sem, ar_send, ar_recv, t_send, t_recv, ta_send, ta_recv, r_send, r_recv, a_send, a_recv,
 ):
     row = lax.axis_index("row")
@@ -138,8 +137,12 @@
     xhi, zhi = x // 2, z // 2
     bit = ((x + xhi) % 2, xhi, (z + zhi) % 2, zhi)
 
-    w_copy = pltpu.make_async_copy(w_hbm, w_ref.at[:, pl.ds(0, COLS)], w_sem)
-    w_copy.start()
+    def load(j):
+        at = pl.ds(pl.multiple_of((y + 1 + j) % 4 * 2 * TALL, 2 * TALL), 2 * TALL)
+        return pltpu.make_async_copy(w_hbm.at[at, :], w_ref.at[at, pl.ds(0, COLS)], w_sem.at[j])
+
+    for j in range(4):
+        load(j).start()
 
     barrier = pltpu.get_barrier_semaphore()
     for d in range(1, NCOL):
@@ -151,7 +154,6 @@
     fac[pl.ds(0, COLS), :] = sketch_ref[...]
     fac[pl.ds(COLS, PAD - COLS), :] = jnp.zeros((PAD - COLS, RANK), bf16)
     pl.semaphore_wait(barrier, NCOL + NROW - 2)
-    w_copy.wait()
 
     def send(src, dst, send_sem, recv_sem, to):
         pltpu.make_async_remote_copy(
@@ -161,57 +163,65 @@
     def wait(ref, sem):
         pltpu.make_async_copy(ref, ref, sem).wait()
 
-    def all_reduce(index):
-        first, second, third = ar1.at[index], ar2.at[index], ar3.at[index]
+    mine16 = pl.ds(pl.multiple_of(col * SEG, SEG), SEG)
+
+    def sum_start(index):
         for d in range(1, NCOL):
             peer = (col + d) % NCOL
-            send(g_ref.at[pl.ds(pl.multiple_of(peer * SEG, SEG), SEG), :], first.at[col],
+            send(g_ref.at[index, pl.ds(pl.multiple_of(peer * SEG, SEG), SEG), :], ar1.at[index, col],
                  ar_send.at[index, 0], ar_recv.at[index, 0], {"col": peer})
-        mine = pl.ds(pl.multiple_of(col * SEG, SEG), SEG)
-        first[col] = g_ref[mine, :]
-        wait(first.at[pl.ds(0, NCOL - 1)], ar_recv.at[index, 0])
-        second[row] = jnp.sum(first[...], axis=0)
+        ar1[index, col] = g_ref[index, mine16, :]
+
+    def sum_row(index):
+        wait(ar1.at[index, pl.ds(0, NCOL - 1)], ar_recv.at[index, 0])
+        ar2[index, row] = jnp.sum(ar1[index], axis=0)
         for d in range(1, NROW):
-            send(second.at[row], second.at[row], ar_send.at[index, 1], ar_recv.at[index, 1],
+            send(ar2.at[index, row], ar2.at[index, row], ar_send.at[index, 1], ar_recv.at[index, 1],
                  {"row": (row + d) % NROW})
-        wait(second.at[pl.ds(0, NROW - 1)], ar_recv.at[index, 1])
-        third[mine, :] = jnp.sum(second[...], axis=0)
+
+    def sum_col(index):
+        wait(ar2.at[index, pl.ds(0, NROW - 1)], ar_recv.at[index, 1])
+        ar3[index, mine16, :] = jnp.sum(ar2[index], axis=0)
         for d in range(1, NCOL):
-            send(third.at[mine, :], third.at[mine, :], ar_send.at[index, 2], ar_recv.at[index, 2],
+            send(ar3.at[index, mine16, :], ar3.at[index, mine16, :], ar_send.at[index, 2], ar_recv.at[index, 2],
                  {"col": (col + d) % NCOL})
-        wait(third.at[pl.ds(0, SEG * (NCOL - 1)), :], ar_recv.at[index, 2])
-        wait(first.at[pl.ds(0, NCOL - 1)], ar_send.at[index, 0])
-        wait(second.at[pl.ds(0, NROW - 1)], ar_send.at[index, 1])
-        wait(third.at[pl.ds(0, SEG * (NCOL - 1)), :], ar_send.at[index, 2])
-
-    def orth(rows, base, hook):
-        def one(turn, carry):
-            panel = own[pl.ds(0, rows), :]
-            g_ref[...] = gram_of(panel)
-            all_reduce(base + turn)
-            cholesky_inverse(ar3[base + turn], s_ref, m_ref, lambda k: hook(turn, k))
-            inverse = m_ref[...]
-
-            @pl.when(turn == 0)
-            def _():
-                total_ref[...] = inverse.T
-                own[pl.ds(0, rows), :] = mm(own[pl.ds(0, rows), :], inverse.T)
-
-            @pl.when(turn == 1)
-            def _():
-                total_ref[...] = mm(total_ref[...], inverse.T)
-
-            return carry
-
-        lax.fori_loop(0, 2, one, 0)
+
+    def sum_end(index):
+        wait(ar3.at[index, pl.ds(0, SEG * (NCOL - 1)), :], ar_recv.at[index, 2])
+        wait(ar1.at[index, pl.ds(0, NCOL - 1)], ar_send.at[index, 0])
+        wait(ar2.at[index, pl.ds(0, NROW - 1)], ar_send.at[index, 1])
+        wait(ar3.at[index, pl.ds(0, SEG * (NCOL - 1)), :], ar_send.at[index, 2])
+
+    def first_pass(index, rows, second_index):
+        second = second_ref[...]
+        gram = mm(mm(second, ar3[index]), second.T)
+        cholesky_inverse(gram, s_ref, m_ref)
+        total = mm(m_ref[...], second).T
+        total_ref[...] = total
+        g_ref[second_index] = gram_of(mm(own[pl.ds(0, rows), :], total))
+        sum_start(second_index)
+
+    def second_pass(index):
+        sum_end(index)
+        cholesky_inverse(ar3[index], s_ref, second_ref)
+
+    second_ref[...] = eye_of()
 
     def step(k, carry):
+        first_tall, second_tall, first_wide, second_wide = (k * 4 + i for i in range(4))
+        last_wide = jnp.maximum(k - 1, 0) * 4 + 3
+
         mine = pl.ds(pl.multiple_of(col * TALL, TALL), TALL)
         tall_k = tall_in.at[k]
 
         def tall_pair(j, carry):
             pair = (y + 1 + j) % 4
             at = pl.ds(pl.multiple_of(pair * 2 * TALL, 2 * TALL), 2 * TALL)
+
+            @pl.when(k == 0)
+            def _():
+                load(j).wait()
+
             y_ref[at, :] = jnp.dot(w_ref[at, :], fac[...], preferred_element_type=f32)
 
             @pl.when(j < 3)
@@ -228,25 +238,37 @@
         send(y_ref.at[pl.ds(pl.multiple_of(peer * TALL, TALL), TALL), :], tall_k.at[col],
              t_send.at[k], t_recv.at[k], {"col": peer})
         tall_k[col] = y_ref[mine, :]
+
+        @pl.when(k > 0)
+        def _():
+            sum_row(last_wide)
+
         wait(tall_k.at[pl.ds(0, NCOL - 1)], t_recv.at[k])
-        wait(tall_k.at[pl.ds(0, NCOL - 1)], t_send.at[k])
         panel = jnp.sum(tall_k[...], axis=0)
         own[pl.ds(0, TALL), :] = panel
+        g_ref[first_tall] = gram_of(panel)
+        sum_start(first_tall)
+        wait(tall_k.at[pl.ds(0, NCOL - 1)], t_send.at[k])
         whole = tall_all.at[k]
         whole[mine, :] = panel
 
-        def tall_hook(turn, block):
-            if block == 0:
-
-                @pl.when(turn == 0)
-                def _():
-                    for d in range(1, NCOL):
-                        send(whole.at[mine, :], whole.at[mine, :], ta_send.at[k], ta_recv.at[k],
-                             {"col": (col + d) % NCOL})
-
-        orth(TALL, k * 4, tall_hook)
+        @pl.when(k > 0)
+        def _():
+            sum_col(last_wide)
+
+        sum_row(first_tall)
+        for d in range(1, NCOL):
+            send(whole.at[mine, :], whole.at[mine, :], ta_send.at[k], ta_recv.at[k],
+                 {"col": (col + d) % NCOL})
+
+        @pl.when(k > 0)
+        def _():
+            second_pass(last_wide)
+
+        sum_col(first_tall)
+        sum_end(first_tall)
+        first_pass(first_tall, TALL, second_tall)
         wait(whole.at[pl.ds(0, TALL * (NCOL - 1)), :], ta_recv.at[k])
-        wait(whole.at[pl.ds(0, TALL * (NCOL - 1)), :], ta_send.at[k])
 
         def make_basis(t, carry):
             at = pl.ds(pl.multiple_of(t * 256, 256), 256)
@@ -256,6 +278,7 @@
             return carry
 
         lax.fori_loop(0, ROWS // 256, make_basis, 0)
+        wait(whole.at[pl.ds(0, TALL * (NCOL - 1)), :], ta_send.at[k])
 
         buffers = (rb0.at[k], rb1.at[k], rb2.at[k], rb3.at[k])
         start = [PART * q for q in range(4)]
@@ -284,13 +307,16 @@
                 start[q] = start[q] + bit[kind] * size
                 if s == 0:
                     times(pl.ds(pl.multiple_of(start[q], 128), size))
+            if s == 0:
+                sum_row(second_tall)
+            if s == 1:
+                sum_col(second_tall)
+            if s == 2:
+                second_pass(second_tall)
             for q in range(4):
                 at = rows_at(start[q], size)
                 wait(buffers[s].at[q], r_recv.at[k, s, q])
                 part[at, :] = part[at, :] + buffers[s][q]
-        for s in range(4):
-            for q in range(4):
-                wait(buffers[s].at[q], r_send.at[k, s, q])
         wide_k = wide_all.at[k]
         for q in range(4):
             at = rows_at(start[q], PIECE)
@@ -316,25 +342,25 @@
                 wait(ref, a_recv.at[k, j, q])
                 wait(ref, a_send.at[k, j, q])
 
+        gather_start(0)
+        g_ref[first_wide] = gram_of(own[...])
+        sum_start(first_wide)
+        for s in range(4):
+            for q in range(4):
+                wait(buffers[s].at[q], r_send.at[k, s, q])
+        sum_row(first_wide)
+        gather_wait(0)
+        gather_start(1)
+        sum_col(first_wide)
+        gather_wait(1)
+        gather_start(2)
+        sum_end(first_wide)
+
         @pl.when(k < POWER)
         def _():
-            def wide_hook(turn, block):
-                if block in (0, 5, 10):
-
-                    @pl.when(turn == 0)
-                    def _():
-                        if block:
-                            gather_wait(block // 5 - 1)
-                        gather_start(block // 5)
-
-                if block == 0:
-
-                    @pl.when(turn == 1)
-                    def _():
-                        gather_wait(2)
-                        gather_start(3)
-
-            orth(OWN, k * 4 + 2, wide_hook)
+            first_pass(first_wide, OWN, second_wide)
+            gather_wait(2)
+            gather_start(3)
             gather_wait(3)
 
             def make_factor(t, carry):
@@ -346,9 +372,6 @@
 
         @pl.when(k == POWER)
         def _():
-            g_ref[...] = gram_of(own[...])
-            all_reduce(k * 4 + 2)
-            gather_start(0)
             eye = eye_of()
 
             def newton(_, pair):
@@ -359,20 +382,21 @@
             def sqrt_pair(matrix, hook):
                 scale = jnp.sqrt(jnp.sum(matrix * matrix, keepdims=True))
                 pair = (matrix / scale, eye)
-                for third in range(3):
-                    pair = lax.fori_loop(0, NS_ITERS // 3, newton, pair)
-                    hook(third)
+                pair = lax.fori_loop(0, NS_ITERS // 3, newton, pair)
+                hook()
+                pair = lax.fori_loop(0, NS_ITERS - NS_ITERS // 3, newton, pair)
                 root = jnp.sqrt(scale)
                 return pair[0] * root, pair[1] / root
 
-            def first(third):
-                gather_wait(third)
-                gather_start(third + 1)
-
-            half, _ = sqrt_pair(ar3[k * 4 + 2], first)
-            quarter, inv_quarter = sqrt_pair(half, lambda third: None)
-            q_ref[...] = quarter
-            iq_ref[...] = inv_quarter
+            def last_gather():
+                gather_wait(2)
+                gather_start(3)
+
+            second = second_ref[...]
+            half, _ = sqrt_pair(mm(mm(second, ar3[first_wide]), second.T), last_gather)
+            quarter, inv_quarter = sqrt_pair(half, lambda: None)
+            q_ref[...] = mm(second.T, quarter)
+            iq_ref[...] = mm(inv_quarter, second)
             gather_wait(3)
             wide_ref[...] = wide_k[...]
 
@@ -408,15 +432,16 @@
             pltpu.VMEM((STEPS, 4, PART // 16, RANK), f32),
             pltpu.VMEM((STEPS, PAD, RANK), f32),
             pltpu.VMEM((OWN, RANK), f32),
-            pltpu.VMEM((RANK, RANK), f32),
+            pltpu.VMEM((STEPS * 4, RANK, RANK), f32),
             pltpu.VMEM((STEPS * 4, NCOL, SEG, RANK), f32),
             pltpu.VMEM((STEPS * 4, NROW, SEG, RANK), f32),
             pltpu.VMEM((STEPS * 4, RANK, RANK), f32),
             pltpu.VMEM((RANK, 2 * RANK), f32),
             pltpu.VMEM((RANK, RANK), f32),
             pltpu.VMEM((RANK, RANK), f32),
+            pltpu.VMEM((RANK, RANK), f32),
             pltpu.VMEM((ROWS, RANK), f32),
-            dma,
+            dma((4,)),
             dma((STEPS * 4, 3)),
             dma((STEPS * 4, 3)),
             dma((STEPS,)),

time: 389 us -> 311 us (0.80)
  Pallas kernels: 386 us -> 309 us
    pallas_call x1, Pallas kernels: 367 us -> 290 us  [factors(): pl.pallas_call(factors_kernel, name='factors', out_shape=(jax.ShapeDtypeS...]
where the time goes in v2:
time: 311 us; the launch traced here: 310 us
  Pallas kernels  309 us (99%)
    pallas_call x1, Pallas kernels, factors(): pl.pallas_call(factors_kernel, name='factors', out_shape=(jax.ShapeDtypeS...  290 us
    pallas_call x1, Pallas kernels, residual(): pl.pallas_call(residual_kernel, name='residual', grid=(COLS // TILE,), ou...  19.5 us

profile of v2, /device:TPU:1, one launch (start us, length us, event | category | flops | bytes accessed | tf_op | source)
XLA Modules:
  0.0 310.0 jit_solution(9335485055709564460)
XLA Ops:
  0.6 289.9 %factors.1 = (f32[1024,128]{1,0:T(8,128)}, f32[5120,128]{1,0:T(8,128)}, f32[128,128]{1,0:T(8,128)}, f32[128,128]{1,0:T(8,128)}) custom-call(bf16[1024,4992]{1,0:T(8,128)(2,1)} %w_ref.1, bf16[4992,128]{1,0:T(8,128)(2,1)} %sketch_ref.1), custom_call_target="tpu_custom_call" | custom-call | tf_op jit(solution)/shard_map/factors/pallas_call | solution.py:411
  290.6 19.5 %residual.1 = (f32[1024,128]{1,0:T(8,128)}, f32[128,4992]{1,0:T(8,128)}, bf16[1024,4992]{1,0:T(8,128)(2,1)}) custom-call(bf16[1024,4992]{1,0:T(8,128)(2,1)} %w_ref.1, f32[1024,128]{1,0:T(8,128)} %get-tuple-element.7.basis_ref, f32[128,128]{1,0:T(8,128)} %get-tuple-element.8.q_ref, f32[128,128]{1,0:T(8,128)} %get-tuple-element.9.iq_ref, ...), custom_call_target="tpu_custom_call" | custom-call | tf_op jit(solution)/shard_map/residual/pallas_call | solution.py:485

commit v3 on v2

v3 whole, which is shorter than its diff:
```python
import jax
import jax.numpy as jnp
from jax import lax
from jax.experimental import pallas as pl
from jax.experimental.pallas import tpu as pltpu
from jax.sharding import PartitionSpec as P

POWER = 2
NS_ITERS = 12
RANK = 128
ROWS = 1024
COLS = 4992
PAD = 5120
NCOL = 8
NROW = 16
PART = PAD // 4
OWN = PAD // NROW
PIECE = PART // NROW
TALL = ROWS // NCOL
SEG = RANK // NCOL
STEPS = POWER + 1
TILE = 384
BLOCK = 32
WIDE_TILES = 3
WIDE_TILE = COLS // WIDE_TILES

f32 = jnp.float32
bf16 = jnp.bfloat16
MESH = pl.DeviceIdType.MESH

ORDER = ((0, 2, 1, 3), (2, 1, 3, 0), (1, 3, 0, 2), (3, 0, 2, 1))


def split3(a):
    hi = a.astype(bf16)
    rest = a - hi.astype(f32)
    mid = rest.astype(bf16)
    low = (rest - mid.astype(f32)).astype(bf16)
    return hi, mid, low


def left6(a, axis):
    hi, mid, low = split3(a)
    return jnp.concatenate([hi, hi, mid, hi, low, mid], axis)


def right6(a, axis):
    hi, mid, low = split3(a)
    return jnp.concatenate([hi, mid, hi, low, hi, mid], axis)


def mm(a, b):
    return jnp.dot(left6(a, 1), right6(b, 0), preferred_element_type=f32)


def gram_of(y):
    return lax.dot_general(
        left6(y, 0), right6(y, 0), (((0,), (0,)), ((), ())), preferred_element_type=f32
    )


def eye_of():
    r = lax.broadcasted_iota(jnp.int32, (RANK, RANK), 0)
    c = lax.broadcasted_iota(jnp.int32, (RANK, RANK), 1)
    return jnp.where(r == c, 1.0, 0.0).astype(f32)


def newton_step(pair, eye):
    upper, inverse = pair
    middle = 1.5 * eye - 0.5 * mm(inverse, upper)
    return mm(upper, middle), mm(middle, inverse)


def cholesky_inverse(gram, s_ref, m_ref):
    s_ref[:, 0:RANK] = gram
    s_ref[:, RANK:] = eye_of()
    sub = lax.broadcasted_iota(jnp.int32, (8, RANK), 0)
    lane = lax.broadcasted_iota(jnp.int32, (BLOCK, RANK), 1)
    groups = range(BLOCK // 8)

    def spread(v, at):
        return jnp.broadcast_to(v[at : at + 1, :], (8, RANK))

    for o in range(0, RANK, BLOCK):
        u = [s_ref[o + 8 * g : o + 8 * g + 8, 0:RANK] for g in groups]
        n = [s_ref[o + 8 * g : o + 8 * g + 8, RANK:] for g in groups]
        square = [
            [jnp.broadcast_to(u[g][:, o + j : o + j + 1], (8, RANK)) if g >= j // 8 else None for g in groups]
            for j in range(BLOCK)
        ]
        scale = [jnp.ones((8, RANK), f32) for _ in groups]
        for j in range(BLOCK):
            top, at = divmod(j, 8)
            pivot = spread(square[j][top], at)
            inverse = 1.0 / pivot
            scale[top] = jnp.where(sub == at, lax.rsqrt(pivot), scale[top])
            u_row, n_row = spread(u[top], at), spread(n[top], at)
            times = {}
            for g in groups[top:]:
                column = square[j][g]
                if g == top:
                    column = jnp.where(sub > at, column, 0.0)
                times[g] = column * inverse
            for c in range(j + 1, BLOCK):
                entry = spread(square[j][c // 8], c % 8)
                for g in groups[c // 8 :]:
                    square[c][g] = square[c][g] - times[g] * entry
            for g in groups[top:]:
                u[g] = u[g] - times[g] * u_row
                n[g] = n[g] - times[g] * n_row
        u = jnp.concatenate([a * b for a, b in zip(u, scale)], 0)
        n = jnp.concatenate([a * b for a, b in zip(n, scale)], 0)
        m_ref[o : o + BLOCK, :] = n
        if o + BLOCK < RANK:
            u = jnp.where(lane >= o + BLOCK, u, 0.0)
            parts = []
            for v in (u, n):
                hi = v.astype(bf16).astype(f32)
                mid = (v - hi).astype(bf16).astype(f32)
                parts.append((hi, mid, v - hi - mid))
            (uh, um, ul), (nh, nm, nl) = parts
            left = jnp.concatenate([uh, uh, um, uh, ul, um], 0)
            right = jnp.concatenate(
                [
                    jnp.concatenate([uh, um, uh, ul, uh, um], 0),
                    jnp.concatenate([nh, nm, nh, nl, nh, nm], 0),
                ],
                1,
            )
            change = lax.dot_general(
                left, right, (((0,), (0,)), ((), ())), preferred_element_type=f32
            )
            s_ref[o + BLOCK :, :] = s_ref[o + BLOCK :, :] - change[o + BLOCK :, :]


def factors_kernel(
    w_hbm, sketch_ref, basis_ref, wide_ref, half_ref, total_ref,
    w_ref, fac, b16, part, tall_in, tall_all, rb0, rb1, rb2, rb3, wide_all,
    own, g_ref, ar1, ar2, ar3, s_ref, m_ref, tall_own, tall_first, tall_second, wide_second, y_ref,
    w_sem, ar_send, ar_recv, t_send, t_recv, ta_send, ta_recv, r_send, r_recv, a_send, a_recv,
):
    row = lax.axis_index("row")
    col = lax.axis_index("col")
    y = col // 2
    x = row // 4
    z = row % 4
    partner = ((x + 1 - 2 * (x % 2)) * 4 + z, (3 - x) * 4 + z, x * 4 + z + 1 - 2 * (z % 2), x * 4 + 3 - z)
    xhi, zhi = x // 2, z // 2
    bit = ((x + xhi) % 2, xhi, (z + zhi) % 2, zhi)

    def load(j):
        at = pl.ds(pl.multiple_of((y + 1 + j) % 4 * 2 * TALL, 2 * TALL), 2 * TALL)
        return pltpu.make_async_copy(w_hbm.at[at, :], w_ref.at[at, pl.ds(0, COLS)], w_sem.at[j])

    for j in range(4):
        load(j).start()

    barrier = pltpu.get_barrier_semaphore()
    for d in range(1, NCOL):
        pl.semaphore_signal(barrier, inc=1, device_id={"col": (col + d) % NCOL}, device_id_type=MESH)
    for d in range(1, NROW):
        pl.semaphore_signal(barrier, inc=1, device_id={"row": (row + d) % NROW}, device_id_type=MESH)

    w_ref[:, pl.ds(COLS, PAD - COLS)] = jnp.zeros((ROWS, PAD - COLS), bf16)
    fac[pl.ds(0, COLS), :] = sketch_ref[...]
    fac[pl.ds(COLS, PAD - COLS), :] = jnp.zeros((PAD - COLS, RANK), bf16)
    pl.semaphore_wait(barrier, NCOL + NROW - 2)

    def send(src, dst, send_sem, recv_sem, to):
        pltpu.make_async_remote_copy(
            src_ref=src, dst_ref=dst, send_sem=send_sem, recv_sem=recv_sem, device_id=to, device_id_type=MESH
        ).start()

    def wait(ref, sem):
        pltpu.make_async_copy(ref, ref, sem).wait()

    mine16 = pl.ds(pl.multiple_of(col * SEG, SEG), SEG)

    def sum_start(index):
        for d in range(1, NCOL):
            peer = (col + d) % NCOL
            send(g_ref.at[index, pl.ds(pl.multiple_of(peer * SEG, SEG), SEG), :], ar1.at[index, col],
                 ar_send.at[index, 0], ar_recv.at[index, 0], {"col": peer})
        ar1[index, col] = g_ref[index, mine16, :]

    def sum_row(index):
        wait(ar1.at[index, pl.ds(0, NCOL - 1)], ar_recv.at[index, 0])
        ar2[index, row] = jnp.sum(ar1[index], axis=0)
        for d in range(1, NROW):
            send(ar2.at[index, row], ar2.at[index, row], ar_send.at[index, 1], ar_recv.at[index, 1],
                 {"row": (row + d) % NROW})

    def sum_col(index):
        wait(ar2.at[index, pl.ds(0, NROW - 1)], ar_recv.at[index, 1])
        ar3[index, mine16, :] = jnp.sum(ar2[index], axis=0)
        for d in range(1, NCOL):
            send(ar3.at[index, mine16, :], ar3.at[index, mine16, :], ar_send.at[index, 2], ar_recv.at[index, 2],
                 {"col": (col + d) % NCOL})

    def sum_end(index):
        wait(ar3.at[index, pl.ds(0, SEG * (NCOL - 1)), :], ar_recv.at[index, 2])
        wait(ar1.at[index, pl.ds(0, NCOL - 1)], ar_send.at[index, 0])
        wait(ar2.at[index, pl.ds(0, NROW - 1)], ar_send.at[index, 1])
        wait(ar3.at[index, pl.ds(0, SEG * (NCOL - 1)), :], ar_send.at[index, 2])

    def corrected(index, before):
        return mm(mm(before, ar3[index]), before.T)

    wide_second[...] = eye_of()

    def step(k, carry):
        first_tall, second_tall, first_wide, second_wide = (k * 4 + i for i in range(4))
        last_wide = jnp.maximum(k - 1, 0) * 4 + 3

        mine = pl.ds(pl.multiple_of(col * TALL, TALL), TALL)
        tall_k = tall_in.at[k]

        def tall_pair(j, carry):
            pair = (y + 1 + j) % 4
            at = pl.ds(pl.multiple_of(pair * 2 * TALL, 2 * TALL), 2 * TALL)

            @pl.when(k == 0)
            def _():
                load(j).wait()

            y_ref[at, :] = jnp.dot(w_ref[at, :], fac[...], preferred_element_type=f32)

            @pl.when(j < 3)
            def _():
                for core in range(2):
                    peer = pair * 2 + core
                    send(y_ref.at[pl.ds(pl.multiple_of(peer * TALL, TALL), TALL), :], tall_k.at[col],
                         t_send.at[k], t_recv.at[k], {"col": peer})

            return carry

        lax.fori_loop(0, 4, tall_pair, 0)
        peer = col + 1 - 2 * (col % 2)
        send(y_ref.at[pl.ds(pl.multiple_of(peer * TALL, TALL), TALL), :], tall_k.at[col],
             t_send.at[k], t_recv.at[k], {"col": peer})
        tall_k[col] = y_ref[mine, :]

        @pl.when(k > 0)
        def _():
            sum_row(last_wide)

        wait(tall_k.at[pl.ds(0, NCOL - 1)], t_recv.at[k])
        panel = jnp.sum(tall_k[...], axis=0)
        whole = tall_all.at[k]
        whole[mine, :] = panel
        for d in range(1, NCOL):
            send(whole.at[mine, :], whole.at[mine, :], ta_send.at[k], ta_recv.at[k],
                 {"col": (col + d) % NCOL})
        tall_own[...] = panel
        g_ref[first_tall] = gram_of(panel)
        sum_start(first_tall)

        @pl.when(k > 0)
        def _():
            sum_col(last_wide)

        wait(whole.at[pl.ds(0, TALL * (NCOL - 1)), :], ta_recv.at[k])
        raw = whole[...]
        high = raw.astype(bf16)
        b16[:, 0:RANK] = high
        b16[:, RANK:] = (raw - high.astype(f32)).astype(bf16)

        buffers = (rb0.at[k], rb1.at[k], rb2.at[k], rb3.at[k])
        start = [PART * q for q in range(4)]

        def times(at):
            both = lax.dot_general(
                w_ref[:, at], b16[...], (((0,), (0,)), ((), ())), preferred_element_type=f32
            )
            part[at, :] = both[:, 0:RANK] + both[:, RANK:]

        def rows_at(offset, size):
            return pl.ds(pl.multiple_of(offset, PIECE), size)

        size = PART
        for s in range(3):
            size = size // 2
            for q in range(4):
                kind = ORDER[q][s]
                at = rows_at(start[q] + (1 - bit[kind]) * size, size)
                if s == 0:
                    at = pl.ds(pl.multiple_of(start[q] + (1 - bit[kind]) * size, 128), size)
                    times(at)
                send(part.at[at, :], buffers[s].at[q], r_send.at[k, s, q], r_recv.at[k, s, q],
                     {"row": partner[kind]})
            for q in range(4):
                kind = ORDER[q][s]
                start[q] = start[q] + bit[kind] * size
                if s == 0:
                    times(pl.ds(pl.multiple_of(start[q], 128), size))
            if s == 0:
                sum_row(first_tall)

                @pl.when(k > 0)
                def _():
                    sum_end(last_wide)
                    cholesky_inverse(ar3[last_wide], s_ref, wide_second)

            if s == 1:
                sum_col(first_tall)
            if s == 2:
                sum_end(first_tall)
                cholesky_inverse(corrected(first_tall, wide_second[...]), s_ref, m_ref)
                tall_first[...] = mm(m_ref[...], wide_second[...])
                g_ref[second_tall] = gram_of(mm(tall_own[...], tall_first[...].T))
                sum_start(second_tall)
            for q in range(4):
                at = rows_at(start[q], size)
                wait(buffers[s].at[q], r_recv.at[k, s, q])
                part[at, :] = part[at, :] + buffers[s][q]
        wide_k = wide_all.at[k]
        for q in range(4):
            send(part.at[rows_at(start[q], size), :], buffers[3].at[q], r_send.at[k, 3, q], r_recv.at[k, 3, q],
                 {"row": partner[ORDER[q][3]]})
        sum_row(second_tall)
        for q in range(4):
            at = rows_at(start[q], size)
            wait(buffers[3].at[q], r_recv.at[k, 3, q])
            wide_k[at, :] = part[at, :] + buffers[3][q]
        for q in range(4):
            at = rows_at(start[q] + bit[ORDER[q][3]] * PIECE, PIECE)
            own[pl.ds(PIECE * q, PIECE), :] = wide_k[at, :]

        place = [list(start)]
        for j in range(3):
            now = list(place[-1])
            for q in range(4):
                now[q] = now[q] - bit[ORDER[q][2 - j]] * (size << j)
            place.append(now)

        def gather_start(j):
            for q in range(4):
                at = rows_at(place[j][q], size << j)
                send(wide_k.at[at, :], wide_k.at[at, :], a_send.at[k, j, q], a_recv.at[k, j, q],
                     {"row": partner[ORDER[q][2 - j]]})

        def gather_wait(j):
            for q in range(4):
                ref = wide_k.at[pl.ds(0, size << j), :]
                wait(ref, a_recv.at[k, j, q])
                wait(ref, a_send.at[k, j, q])

        gather_start(0)
        own[...] = mm(own[...], tall_first[...].T)
        g_ref[first_wide] = gram_of(own[...])
        sum_start(first_wide)
        wait(tall_k.at[pl.ds(0, NCOL - 1)], t_send.at[k])
        wait(whole.at[pl.ds(0, TALL * (NCOL - 1)), :], ta_send.at[k])
        for s in range(4):
            for q in range(4):
                wait(buffers[s].at[q], r_send.at[k, s, q])
        sum_col(second_tall)
        sum_row(first_wide)
        gather_wait(0)
        gather_start(1)
        sum_end(second_tall)
        cholesky_inverse(ar3[second_tall], s_ref, tall_second)
        sum_col(first_wide)
        gather_wait(1)
        gather_start(2)
        second = tall_second[...]
        total = mm(second, tall_first[...])
        sum_end(first_wide)
        gram = corrected(first_wide, second)

        @pl.when(k < POWER)
        def _():
            cholesky_inverse(gram, s_ref, m_ref)
            inverse = m_ref[...]
            turned = mm(inverse, total).T
            g_ref[second_wide] = gram_of(mm(own[...], mm(inverse, second).T))
            sum_start(second_wide)
            gather_wait(2)
            right = right6(turned, 0)

            def make_factor(t, carry):
                at = pl.ds(pl.multiple_of(t * 512, 512), 512)
                fac[at, :] = jnp.dot(left6(wide_k[at, :], 1), right, preferred_element_type=f32).astype(bf16)
                return carry

            lax.fori_loop(0, PAD // 512, make_factor, 0)

        @pl.when(k == POWER)
        def _():
            eye = eye_of()
            scale = jnp.sqrt(jnp.sum(gram * gram, keepdims=True))

            def newton(_, pair):
                return newton_step(pair, eye)

            pair = lax.fori_loop(0, NS_ITERS, newton, (gram / scale, eye))
            half_ref[...] = pair[0] * jnp.sqrt(scale)
            total_ref[...] = total
            basis_ref[...] = whole[...]
            gather_wait(2)
            wide_ref[...] = wide_k[...]

        return carry

    lax.fori_loop(0, STEPS, step, 0)


def factors(weight, sketch):
    vmem = pl.BlockSpec(memory_space=pltpu.VMEM)
    dma = pltpu.SemaphoreType.DMA
    return pl.pallas_call(
        factors_kernel,
        name="factors",
        out_shape=(
            jax.ShapeDtypeStruct((ROWS, RANK), f32),
            jax.ShapeDtypeStruct((PAD, RANK), f32),
            jax.ShapeDtypeStruct((RANK, RANK), f32),
            jax.ShapeDtypeStruct((RANK, RANK), f32),
        ),
        in_specs=[pl.BlockSpec(memory_space=pl.ANY), vmem],
        out_specs=(vmem, vmem, vmem, vmem),
        scratch_shapes=[
            pltpu.VMEM((ROWS, PAD), bf16),
            pltpu.VMEM((PAD, RANK), bf16),
            pltpu.VMEM((ROWS, 2 * RANK), bf16),
            pltpu.VMEM((PAD, RANK), f32),
            pltpu.VMEM((STEPS, NCOL, TALL, RANK), f32),
            pltpu.VMEM((STEPS, ROWS, RANK), f32),
            pltpu.VMEM((STEPS, 4, PART // 2, RANK), f32),
            pltpu.VMEM((STEPS, 4, PART // 4, RANK), f32),
            pltpu.VMEM((STEPS, 4, PART // 8, RANK), f32),
            pltpu.VMEM((STEPS, 4, PART // 8, RANK), f32),
            pltpu.VMEM((STEPS, PAD, RANK), f32),
            pltpu.VMEM((OWN, RANK), f32),
            pltpu.VMEM((STEPS * 4, RANK, RANK), f32),
            pltpu.VMEM((STEPS * 4, NCOL, SEG, RANK), f32),
            pltpu.VMEM((STEPS * 4, NROW, SEG, RANK), f32),
            pltpu.VMEM((STEPS * 4, RANK, RANK), f32),
            pltpu.VMEM((RANK, 2 * RANK), f32),
            pltpu.VMEM((RANK, RANK), f32),
            pltpu.VMEM((TALL, RANK), f32),
            pltpu.VMEM((RANK, RANK), f32),
            pltpu.VMEM((RANK, RANK), f32),
            pltpu.VMEM((RANK, RANK), f32),
            pltpu.VMEM((ROWS, RANK), f32),
            dma((4,)),
            dma((STEPS * 4, 3)),
            dma((STEPS * 4, 3)),
            dma((STEPS,)),
            dma((STEPS,)),
            dma((STEPS,)),
            dma((STEPS,)),
            dma((STEPS, 4, 4)),
            dma((STEPS, 4, 4)),
            dma((STEPS, 3, 4)),
            dma((STEPS, 3, 4)),
        ],
        compiler_params=pltpu.CompilerParams(
            collective_id=0, has_side_effects=True, vmem_limit_bytes=60 << 20
        ),
    )(weight, sketch)


def residual_kernel(
    w_hbm, basis_hbm, wide_hbm, half_ref, total_ref, fa_hbm, fb_hbm, res_hbm,
    w_ref, basis_ref, wide_ref, six, left, right, fa_ref, fb_ref, w_sem, in_sem, fa_sem, fb_sem, res_sem,
):
    wide_load = pltpu.make_async_copy(wide_hbm, wide_ref, in_sem.at[0])
    basis_load = pltpu.make_async_copy(basis_hbm, basis_ref, in_sem.at[1])
    wide_load.start()
    basis_load.start()
    loads = []
    for i in range(4):
        at = pl.ds(i * 256, 256)
        loads.append(pltpu.make_async_copy(w_hbm.at[at, :], w_ref.at[at, :], w_sem.at[i]))
        loads[-1].start()
    wide_load.wait()

    def prepare(t):
        at = pl.ds(pl.multiple_of(t * TILE, 128), TILE)
        six[:, at] = right6(wide_ref[at, :].T, 0)

    eye = eye_of()
    half = half_ref[...]
    scale = jnp.sqrt(jnp.sum(half * half, keepdims=True))

    def newton(i, pair):
        prepare(i)
        return newton_step(pair, eye)

    upper, inverse = lax.fori_loop(0, NS_ITERS, newton, (half / scale, eye))
    prepare(NS_ITERS)
    root = jnp.sqrt(scale)
    total = total_ref[...]
    quarter = mm(total.T, upper * root)
    six_left = left6(mm(inverse / root, total), 1)
    basis_load.wait()
    fa_store = pltpu.make_async_copy(fa_ref, fa_hbm, fa_sem)
    for t in range(ROWS // 256):
        at = pl.ds(t * 256, 256)
        a = mm(basis_ref[at, :], quarter)
        fa_ref[at, :] = a
        hi = a.astype(bf16)
        low = (a - hi.astype(f32)).astype(bf16)
        left[at, :] = jnp.concatenate([hi, low, hi], 1)
    fa_store.start()
    stores = [fa_store]
    for load in loads:
        load.wait()
    for t in range(WIDE_TILES):
        at = pl.ds(t * WIDE_TILE, WIDE_TILE)
        b = jnp.dot(six_left, six[:, at], preferred_element_type=f32)
        fb_ref[:, at] = b
        hi = b.astype(bf16)
        low = (b - hi.astype(f32)).astype(bf16)
        right[:, at] = jnp.concatenate([hi, hi, low], 0)
        stores.append(pltpu.make_async_copy(fb_ref.at[:, at], fb_hbm.at[:, at], fb_sem.at[t]))
        stores[-1].start()
        for r in range(2):
            rows = pl.ds(r * (ROWS // 2), ROWS // 2)
            product = jnp.dot(left[rows, :], right[:, at], preferred_element_type=f32)
            w_ref[rows, at] = (w_ref[rows, at].astype(f32) - product).astype(bf16)
            stores.append(pltpu.make_async_copy(w_ref.at[rows, at], res_hbm.at[rows, at], res_sem.at[t, r]))
            stores[-1].start()
    for store in stores:
        store.wait()


def residual(weight, basis, wide, half, total):
    vmem = pl.BlockSpec(memory_space=pltpu.VMEM)
    hbm = pl.BlockSpec(memory_space=pl.ANY)
    dma = pltpu.SemaphoreType.DMA
    return pl.pallas_call(
        residual_kernel,
        name="residual",
        out_shape=(
            jax.ShapeDtypeStruct((ROWS, RANK), f32),
            jax.ShapeDtypeStruct((RANK, COLS), f32),
            jax.ShapeDtypeStruct((ROWS, COLS), bf16),
        ),
        in_specs=[hbm, hbm, hbm, vmem, vmem],
        out_specs=(hbm, hbm, hbm),
        scratch_shapes=[
            pltpu.VMEM((ROWS, COLS), bf16),
            pltpu.VMEM((ROWS, RANK), f32),
            pltpu.VMEM((PAD, RANK), f32),
            pltpu.VMEM((6 * RANK, COLS), bf16),
            pltpu.VMEM((ROWS, 3 * RANK), bf16),
            pltpu.VMEM((3 * RANK, COLS), bf16),
            pltpu.VMEM((ROWS, RANK), f32),
            pltpu.VMEM((RANK, COLS), f32),
            dma((4,)),
            dma((2,)),
            dma,
            dma((WIDE_TILES,)),
            dma((WIDE_TILES, 2)),
        ],
        compiler_params=pltpu.CompilerParams(vmem_limit_bytes=60 << 20),
    )(weight, basis, wide, half, total)


def on_device(weight, sketch):
    return residual(weight, *factors(weight, sketch))


def solution(mesh):
    return jax.shard_map(
        on_device,
        mesh=mesh,
        in_specs=(P("row", "col"), P("col", None)),
        out_specs=(P("row", None), P(None, "col"), P("row", "col")),
        check_vma=False,
    )
```

time: 311 us -> 241 us (0.77)
  Pallas kernels: 309 us -> 240 us
    pallas_call x1, Pallas kernels: 290 us -> 221 us  [factors(): pl.pallas_call(factors_kernel, name='factors', out_shape=(jax.ShapeDtypeS...]
where the time goes in v3:
time: 241 us
  Pallas kernels  240 us (100%)
    pallas_call x1, Pallas kernels, factors(): pl.pallas_call(factors_kernel, name='factors', out_shape=(jax.ShapeDtypeS...  221 us
    pallas_call x1, Pallas kernels, residual(): pl.pallas_call(residual_kernel, name='residual', out_shape=(jax.ShapeDtyp...  18.8 us

profile of v3, /device:TPU:1, one launch (start us, length us, event | category | flops | bytes accessed | tf_op | source)
XLA Modules:
  0.0 240.5 jit_solution(13998553672483220284)
XLA Ops:
  0.6 220.9 %factors.1 = (f32[1024,128]{1,0:T(8,128)}, f32[5120,128]{1,0:T(8,128)}, f32[128,128]{1,0:T(8,128)}, f32[128,128]{1,0:T(8,128)}) custom-call(bf16[1024,4992]{1,0:T(8,128)(2,1)} %w_hbm.3, bf16[4992,128]{1,0:T(8,128)(2,1)} %sketch_ref.1), custom_call_target="tpu_custom_call" | custom-call | tf_op jit(solution)/shard_map/factors/pallas_call | solution.py:411
  221.6 18.8 %residual.1 = (f32[1024,128]{1,0:T(8,128)}, f32[128,4992]{1,0:T(8,128)}, bf16[1024,4992]{1,0:T(8,128)(2,1)}) custom-call(bf16[1024,4992]{1,0:T(8,128)(2,1)} %w_hbm.3, f32[1024,128]{1,0:T(8,128)} %get-tuple-element.7.basis_hbm, f32[5120,128]{1,0:T(8,128)} %get-tuple-element.8.wide_hbm, f32[128,128]{1,0:T(8,128)} %get-tuple-element.9.half_ref, ...), custom_call_target="tpu_custom_call" | custom-call | tf_op jit(solution)/shard_map/residual/pallas_call | solution.py:533

commit v4 on v3

--- a/solution.py
+++ b/solution.py
@@ -29,6 +29,10 @@
 MESH = pl.DeviceIdType.MESH
 
 ORDER = ((0, 2, 1, 3), (2, 1, 3, 0), (1, 3, 0, 2), (3, 0, 2, 1))
+
+MESSAGES = ((0, 320), (320, 320), (640, 160), (800, 160), (960, 160), (1120, 160))
+LOW_FROM = (POWER, POWER, POWER, POWER, 0, 0)
+GATHER = (2, 1, 0, 1, 0, 0)
 
 
 def split3(a):
@@ -135,9 +139,9 @@
 
 def factors_kernel(
     w_hbm, sketch_ref, basis_ref, wide_ref, half_ref, total_ref,
-    w_ref, fac, b16, part, tall_in, tall_all, rb0, rb1, rb2, rb3, wide_all,
+    w_ref, fac, b16, part, core_in, core_sum, tall_in, tall_all, stage_hi, stage_lo, land_hi, land_lo, wide_all,
     own, g_ref, ar1, ar2, ar3, s_ref, m_ref, tall_own, tall_first, tall_second, wide_second, y_ref,
-    w_sem, ar_send, ar_recv, t_send, t_recv, ta_send, ta_recv, r_send, r_recv, a_send, a_recv,
+    w_sem, ar_send, ar_recv, c_send, c_recv, t_send, t_recv, ta_send, ta_recv, r_send, r_recv, l_send, l_recv, a_send, a_recv,
 ):
     row = lax.axis_index("row")
     col = lax.axis_index("col")
@@ -215,6 +219,12 @@
         mine = pl.ds(pl.multiple_of(col * TALL, TALL), TALL)
         tall_k = tall_in.at[k]
 
+        core = col % 2
+        sibling = {"col": col + 1 - 2 * core}
+
+        def chunk(index):
+            return pl.ds(pl.multiple_of(index * TALL, TALL), TALL)
+
         def tall_pair(j, carry):
             pair = (y + 1 + j) % 4
             at = pl.ds(pl.multiple_of(pair * 2 * TALL, 2 * TALL), 2 * TALL)
@@ -224,33 +234,33 @@
                 load(j).wait()
 
             y_ref[at, :] = jnp.dot(w_ref[at, :], fac[...], preferred_element_type=f32)
-
-            @pl.when(j < 3)
+            send(y_ref.at[chunk(pair * 2 + 1 - core), :], core_in.at[k, j], c_send.at[k, j], c_recv.at[k, j], sibling)
+
+            @pl.when(j > 0)
             def _():
-                for core in range(2):
-                    peer = pair * 2 + core
-                    send(y_ref.at[pl.ds(pl.multiple_of(peer * TALL, TALL), TALL), :], tall_k.at[col],
-                         t_send.at[k], t_recv.at[k], {"col": peer})
+                before = (y + j) % 4 * 2 + core
+                wait(core_in.at[k, j - 1], c_recv.at[k, j - 1])
+                core_sum[j - 1] = y_ref[chunk(before), :] + core_in[k, j - 1]
+                send(core_sum.at[j - 1], tall_k.at[y], t_send.at[k], t_recv.at[k], {"col": before})
 
             return carry
 
         lax.fori_loop(0, 4, tall_pair, 0)
-        peer = col + 1 - 2 * (col % 2)
-        send(y_ref.at[pl.ds(pl.multiple_of(peer * TALL, TALL), TALL), :], tall_k.at[col],
-             t_send.at[k], t_recv.at[k], {"col": peer})
-        tall_k[col] = y_ref[mine, :]
+        wait(core_in.at[k, 3], c_recv.at[k, 3])
+        tall_k[y] = y_ref[mine, :] + core_in[k, 3]
 
         @pl.when(k > 0)
         def _():
             sum_row(last_wide)
 
-        wait(tall_k.at[pl.ds(0, NCOL - 1)], t_recv.at[k])
+        wait(tall_k.at[pl.ds(0, 3)], t_recv.at[k])
         panel = jnp.sum(tall_k[...], axis=0)
         whole = tall_all.at[k]
         whole[mine, :] = panel
-        for d in range(1, NCOL):
-            send(whole.at[mine, :], whole.at[mine, :], ta_send.at[k], ta_recv.at[k],
-                 {"col": (col + d) % NCOL})
+        for d in (1, 3, 2):
+            send(whole.at[mine, :], whole.at[mine, :], ta_send.at[k, 4 - d], ta_recv.at[k, 4 - d],
+                 {"col": (y + d) % 4 * 2 + core})
+        send(whole.at[mine, :], whole.at[mine, :], ta_send.at[k, 0], ta_recv.at[k, 0], sibling)
         tall_own[...] = panel
         g_ref[first_tall] = gram_of(panel)
         sum_start(first_tall)
@@ -259,14 +269,17 @@
         def _():
             sum_col(last_wide)
 
-        wait(whole.at[pl.ds(0, TALL * (NCOL - 1)), :], ta_recv.at[k])
+        for d in (1, 3, 2):
+            at = chunk((y + d) % 4 * 2 + core)
+            wait(whole.at[at, :], ta_recv.at[k, d])
+            send(whole.at[at, :], whole.at[at, :], ta_send.at[k, 4 + d], ta_recv.at[k, 4 + d], sibling)
+        for d in (0, 5, 6, 7):
+            wait(whole.at[mine, :], ta_recv.at[k, d])
+        sum_row(first_tall)
         raw = whole[...]
         high = raw.astype(bf16)
         b16[:, 0:RANK] = high
         b16[:, RANK:] = (raw - high.astype(f32)).astype(bf16)
-
-        buffers = (rb0.at[k], rb1.at[k], rb2.at[k], rb3.at[k])
-        start = [PART * q for q in range(4)]
 
         def times(at):
             both = lax.dot_general(
@@ -277,92 +290,140 @@
         def rows_at(offset, size):
             return pl.ds(pl.multiple_of(offset, PIECE), size)
 
-        size = PART
-        for s in range(3):
-            size = size // 2
+        def post(m, q, kind, offset):
+            start, size = MESSAGES[m]
+            at = rows_at(offset, size)
+            land = pl.ds(start, size)
+            value = part[at, :]
+            high = value.astype(bf16)
+            stage_hi[at, :] = high
+            send(stage_hi.at[at, :], land_hi.at[k, q, land, :], r_send.at[k, m, q], r_recv.at[k, m, q],
+                 {"row": partner[kind]})
+
+            @pl.when(k >= LOW_FROM[m])
+            def _():
+                stage_lo[at, :] = (value - high.astype(f32)).astype(bf16)
+                send(stage_lo.at[at, :], land_lo.at[k, q, land, :], l_send.at[k, m, q], l_recv.at[k, m, q],
+                     {"row": partner[kind]})
+
+        def take(m, q, offset):
+            start, size = MESSAGES[m]
+            at = rows_at(offset, size)
+            land = pl.ds(start, size)
+            wait(land_hi.at[k, q, land, :], r_recv.at[k, m, q])
+            part[at, :] = part[at, :] + land_hi[k, q, land, :].astype(f32)
+
+            @pl.when(k >= LOW_FROM[m])
+            def _():
+                wait(land_lo.at[k, q, land, :], l_recv.at[k, m, q])
+                part[at, :] = part[at, :] + land_lo[k, q, land, :].astype(f32)
+
+        kinds = ORDER
+        half_size, quarter_size, size = PART // 2, PART // 4, PART // 8
+        keep0, keep1, send1, keep2, send2 = [], [], [], [], []
+        for q in range(4):
+            b0, b1, b2 = (bit[kinds[q][s]] for s in range(3))
+            away = PART * q + (1 - b0) * half_size
+            times(pl.ds(pl.multiple_of(away, 128), half_size))
+            post(0, q, kinds[q][0], away + (1 - b1) * quarter_size)
+            post(1, q, kinds[q][0], away + b1 * quarter_size)
+            keep0.append(PART * q + b0 * half_size)
+            send1.append(keep0[q] + (1 - b1) * quarter_size)
+            keep1.append(keep0[q] + b1 * quarter_size)
+            send2.append(keep1[q] + (1 - b2) * size)
+            keep2.append(keep1[q] + b2 * size)
+        for q in range(4):
+            times(pl.ds(pl.multiple_of(keep0[q], 128), half_size))
+
+        @pl.when(k > 0)
+        def _():
+            sum_end(last_wide)
+            cholesky_inverse(ar3[last_wide], s_ref, wide_second)
+
+        for q in range(4):
+            b2 = bit[kinds[q][2]]
+            take(0, q, send1[q])
+            post(2, q, kinds[q][1], send1[q] + (1 - b2) * size)
+            post(3, q, kinds[q][1], send1[q] + b2 * size)
+        sum_col(first_tall)
+        for q in range(4):
+            take(1, q, keep1[q])
+        for q in range(4):
+            take(2, q, send2[q])
+            post(4, q, kinds[q][2], send2[q])
+        sum_end(first_tall)
+        cholesky_inverse(corrected(first_tall, wide_second[...]), s_ref, m_ref)
+        for q in range(4):
+            take(3, q, keep2[q])
+        for q in range(4):
+            take(4, q, keep2[q])
+            post(5, q, kinds[q][3], keep2[q])
+        tall_first[...] = mm(m_ref[...], wide_second[...])
+        g_ref[second_tall] = gram_of(mm(tall_own[...], tall_first[...].T))
+        sum_start(second_tall)
+        wide_k = wide_all.at[k]
+        for q in range(4):
+            at = rows_at(keep2[q], size)
+            land = pl.ds(*MESSAGES[5])
+            wait(land_hi.at[k, q, land, :], r_recv.at[k, 5, q])
+            wide_k[at, :] = stage_hi[at, :].astype(f32) + land_hi[k, q, land, :].astype(f32)
+            wait(land_lo.at[k, q, land, :], l_recv.at[k, 5, q])
+            low = stage_lo[at, :].astype(f32) + land_lo[k, q, land, :].astype(f32)
+            wide_k[at, :] = wide_k[at, :] + low
+
+        for q in range(4):
+            at = rows_at(keep2[q] + bit[kinds[q][3]] * PIECE, PIECE)
+            own[pl.ds(PIECE * q, PIECE), :] = wide_k[at, :]
+
+        def gather(g, offsets, rows):
             for q in range(4):
-                kind = ORDER[q][s]
-                at = rows_at(start[q] + (1 - bit[kind]) * size, size)
-                if s == 0:
-                    at = pl.ds(pl.multiple_of(start[q] + (1 - bit[kind]) * size, 128), size)
-                    times(at)
-                send(part.at[at, :], buffers[s].at[q], r_send.at[k, s, q], r_recv.at[k, s, q],
-                     {"row": partner[kind]})
+                at = rows_at(offsets[q], rows)
+                send(wide_k.at[at, :], wide_k.at[at, :], a_send.at[k, g, q], a_recv.at[k, g, q],
+                     {"row": partner[kinds[q][GATHER[g]]]})
+
+        def gather_wait(g, rows, sem):
             for q in range(4):
-                kind = ORDER[q][s]
-                start[q] = start[q] + bit[kind] * size
-                if s == 0:
-                    times(pl.ds(pl.multiple_of(start[q], 128), size))
-            if s == 0:
-                sum_row(first_tall)
-
-                @pl.when(k > 0)
-                def _():
-                    sum_end(last_wide)
-                    cholesky_inverse(ar3[last_wide], s_ref, wide_second)
-
-            if s == 1:
-                sum_col(first_tall)
-            if s == 2:
-                sum_end(first_tall)
-                cholesky_inverse(corrected(first_tall, wide_second[...]), s_ref, m_ref)
-                tall_first[...] = mm(m_ref[...], wide_second[...])
-                g_ref[second_tall] = gram_of(mm(tall_own[...], tall_first[...].T))
-                sum_start(second_tall)
-            for q in range(4):
-                at = rows_at(start[q], size)
-                wait(buffers[s].at[q], r_recv.at[k, s, q])
-                part[at, :] = part[at, :] + buffers[s][q]
-        wide_k = wide_all.at[k]
-        for q in range(4):
-            send(part.at[rows_at(start[q], size), :], buffers[3].at[q], r_send.at[k, 3, q], r_recv.at[k, 3, q],
-                 {"row": partner[ORDER[q][3]]})
-        sum_row(second_tall)
-        for q in range(4):
-            at = rows_at(start[q], size)
-            wait(buffers[3].at[q], r_recv.at[k, 3, q])
-            wide_k[at, :] = part[at, :] + buffers[3][q]
-        for q in range(4):
-            at = rows_at(start[q] + bit[ORDER[q][3]] * PIECE, PIECE)
-            own[pl.ds(PIECE * q, PIECE), :] = wide_k[at, :]
-
-        place = [list(start)]
-        for j in range(3):
-            now = list(place[-1])
-            for q in range(4):
-                now[q] = now[q] - bit[ORDER[q][2 - j]] * (size << j)
-            place.append(now)
-
-        def gather_start(j):
-            for q in range(4):
-                at = rows_at(place[j][q], size << j)
-                send(wide_k.at[at, :], wide_k.at[at, :], a_send.at[k, j, q], a_recv.at[k, j, q],
-                     {"row": partner[ORDER[q][2 - j]]})
-
-        def gather_wait(j):
-            for q in range(4):
-                ref = wide_k.at[pl.ds(0, size << j), :]
-                wait(ref, a_recv.at[k, j, q])
-                wait(ref, a_send.at[k, j, q])
-
-        gather_start(0)
+                wait(wide_k.at[pl.ds(0, rows), :], sem.at[k, g, q])
+
+        for g in range(3):
+            gather(g, keep2, size)
         own[...] = mm(own[...], tall_first[...].T)
         g_ref[first_wide] = gram_of(own[...])
         sum_start(first_wide)
-        wait(tall_k.at[pl.ds(0, NCOL - 1)], t_send.at[k])
-        wait(whole.at[pl.ds(0, TALL * (NCOL - 1)), :], ta_send.at[k])
-        for s in range(4):
+        sum_row(second_tall)
+        wait(tall_k.at[pl.ds(0, 3)], t_send.at[k])
+        for j in range(4):
+            wait(core_in.at[k, j], c_send.at[k, j])
+        for d in (0, 1, 2, 3, 5, 6, 7):
+            wait(whole.at[mine, :], ta_send.at[k, d])
+        for m, (_, rows) in enumerate(MESSAGES):
             for q in range(4):
-                wait(buffers[s].at[q], r_send.at[k, s, q])
+                wait(stage_hi.at[pl.ds(0, rows), :], r_send.at[k, m, q])
+
+                @pl.when(k >= LOW_FROM[m])
+                def _():
+                    wait(stage_lo.at[pl.ds(0, rows), :], l_send.at[k, m, q])
+
+        sum_row(first_wide)
+        gather_wait(0, size, a_recv)
+        gather(3, send2, size)
+        gather(4, send2, size)
         sum_col(second_tall)
-        sum_row(first_wide)
-        gather_wait(0)
-        gather_start(1)
+        sum_col(first_wide)
+        gather_wait(1, size, a_recv)
+        gather_wait(3, size, a_recv)
+        gather(5, send1, 2 * size)
         sum_end(second_tall)
         cholesky_inverse(ar3[second_tall], s_ref, tall_second)
-        sum_col(first_wide)
-        gather_wait(1)
-        gather_start(2)
+
+        def gather_end():
+            gather_wait(2, size, a_recv)
+            gather_wait(4, size, a_recv)
+            gather_wait(5, 2 * size, a_recv)
+            for g in range(5):
+                gather_wait(g, size, a_send)
+            gather_wait(5, 2 * size, a_send)
+
         second = tall_second[...]
         total = mm(second, tall_first[...])
         sum_end(first_wide)
@@ -375,7 +436,7 @@
             turned = mm(inverse, total).T
             g_ref[second_wide] = gram_of(mm(own[...], mm(inverse, second).T))
             sum_start(second_wide)
-            gather_wait(2)
+            gather_end()
             right = right6(turned, 0)
 
             def make_factor(t, carry):
@@ -397,7 +458,7 @@
             half_ref[...] = pair[0] * jnp.sqrt(scale)
             total_ref[...] = total
             basis_ref[...] = whole[...]
-            gather_wait(2)
+            gather_end()
             wide_ref[...] = wide_k[...]
 
         return carry
@@ -424,12 +485,14 @@
             pltpu.VMEM((PAD, RANK), bf16),
             pltpu.VMEM((ROWS, 2 * RANK), bf16),
             pltpu.VMEM((PAD, RANK), f32),
-            pltpu.VMEM((STEPS, NCOL, TALL, RANK), f32),
+            pltpu.VMEM((STEPS, 4, TALL, RANK), f32),
+            pltpu.VMEM((4, TALL, RANK), f32),
+            pltpu.VMEM((STEPS, 4, TALL, RANK), f32),
             pltpu.VMEM((STEPS, ROWS, RANK), f32),
-            pltpu.VMEM((STEPS, 4, PART // 2, RANK), f32),
-            pltpu.VMEM((STEPS, 4, PART // 4, RANK), f32),
-            pltpu.VMEM((STEPS, 4, PART // 8, RANK), f32),
-            pltpu.VMEM((STEPS, 4, PART // 8, RANK), f32),
+            pltpu.VMEM((PAD, RANK), bf16),
+            pltpu.VMEM((PAD, RANK), bf16),
+            pltpu.VMEM((STEPS, 4, PART, RANK), bf16),
+            pltpu.VMEM((STEPS, 4, PART, RANK), bf16),
             pltpu.VMEM((STEPS, PAD, RANK), f32),
             pltpu.VMEM((OWN, RANK), f32),
             pltpu.VMEM((STEPS * 4, RANK, RANK), f32),
@@ -446,14 +509,18 @@
             dma((4,)),
             dma((STEPS * 4, 3)),
             dma((STEPS * 4, 3)),
+            dma((STEPS, 4)),
+            dma((STEPS, 4)),
             dma((STEPS,)),
             dma((STEPS,)),
-            dma((STEPS,)),
-            dma((STEPS,)),
-            dma((STEPS, 4, 4)),
-            dma((STEPS, 4, 4)),
-            dma((STEPS, 3, 4)),
-            dma((STEPS, 3, 4)),
+            dma((STEPS, 8)),
+            dma((STEPS, 8)),
+            dma((STEPS, 6, 4)),
+            dma((STEPS, 6, 4)),
+            dma((STEPS, 6, 4)),
+            dma((STEPS, 6, 4)),
+            dma((STEPS, 6, 4)),
+            dma((STEPS, 6, 4)),
         ],
         compiler_params=pltpu.CompilerParams(
             collective_id=0, has_side_effects=True, vmem_limit_bytes=60 << 20

time: 241 us -> 223 us (0.925)
  Pallas kernels: 240 us -> 222 us
    pallas_call x1, Pallas kernels: 221 us -> 203 us  [factors(): pl.pallas_call(factors_kernel, name='factors', out_shape=(jax.ShapeDtypeS...]
where the time goes in v4:
time: 223 us
  Pallas kernels  222 us (100%)
    pallas_call x1, Pallas kernels, factors(): pl.pallas_call(factors_kernel, name='factors', out_shape=(jax.ShapeDtypeS...  203 us
    pallas_call x1, Pallas kernels, residual(): pl.pallas_call(residual_kernel, name='residual', out_shape=(jax.ShapeDtyp...  18.8 us

profile of v4, /device:TPU:1, one launch (start us, length us, event | category | flops | bytes accessed | tf_op | source)
XLA Modules:
  0.0 222.9 jit_solution(14141286052236509491)
XLA Ops:
  0.6 203.3 %factors.1 = (f32[1024,128]{1,0:T(8,128)}, f32[5120,128]{1,0:T(8,128)}, f32[128,128]{1,0:T(8,128)}, f32[128,128]{1,0:T(8,128)}) custom-call(bf16[1024,4992]{1,0:T(8,128)(2,1)} %w_hbm.3, bf16[4992,128]{1,0:T(8,128)(2,1)} %sketch_ref.1), custom_call_target="tpu_custom_call" | custom-call | tf_op jit(solution)/shard_map/factors/pallas_call | solution.py:472
  203.9 18.8 %residual.1 = (f32[1024,128]{1,0:T(8,128)}, f32[128,4992]{1,0:T(8,128)}, bf16[1024,4992]{1,0:T(8,128)(2,1)}) custom-call(bf16[1024,4992]{1,0:T(8,128)(2,1)} %w_hbm.3, f32[1024,128]{1,0:T(8,128)} %get-tuple-element.7.basis_hbm, f32[5120,128]{1,0:T(8,128)} %get-tuple-element.8.wide_hbm, f32[128,128]{1,0:T(8,128)} %get-tuple-element.9.half_ref, ...), custom_call_target="tpu_custom_call" | custom-call | tf_op jit(solution)/shard_map/residual/pallas_call | solution.py:600

commit v5 on v4

--- a/solution.py
+++ b/solution.py
@@ -19,7 +19,7 @@
 TALL = ROWS // NCOL
 SEG = RANK // NCOL
 STEPS = POWER + 1
-TILE = 384
+TILE = 512
 BLOCK = 32
 WIDE_TILES = 3
 WIDE_TILE = COLS // WIDE_TILES
@@ -141,7 +141,7 @@
     w_hbm, sketch_ref, basis_ref, wide_ref, half_ref, total_ref,
     w_ref, fac, b16, part, core_in, core_sum, tall_in, tall_all, stage_hi, stage_lo, land_hi, land_lo, wide_all,
     own, g_ref, ar1, ar2, ar3, s_ref, m_ref, tall_own, tall_first, tall_second, wide_second, y_ref,
-    w_sem, ar_send, ar_recv, c_send, c_recv, t_send, t_recv, ta_send, ta_recv, r_send, r_recv, l_send, l_recv, a_send, a_recv,
+    w_sem, out_sem, ar_send, ar_recv, c_send, c_recv, t_send, t_recv, ta_send, ta_recv, r_send, r_recv, l_send, l_recv, a_send, a_recv,
 ):
     row = lax.axis_index("row")
     col = lax.axis_index("col")
@@ -454,12 +454,17 @@
             def newton(_, pair):
                 return newton_step(pair, eye)
 
-            pair = lax.fori_loop(0, NS_ITERS, newton, (gram / scale, eye))
+            basis_store = pltpu.make_async_copy(whole, basis_ref, out_sem.at[0])
+            wide_store = pltpu.make_async_copy(wide_k, wide_ref, out_sem.at[1])
+            basis_store.start()
+            total_ref[...] = total
+            pair = lax.fori_loop(0, NS_ITERS // 2, newton, (gram / scale, eye))
+            gather_end()
+            wide_store.start()
+            pair = lax.fori_loop(0, NS_ITERS - NS_ITERS // 2, newton, pair)
             half_ref[...] = pair[0] * jnp.sqrt(scale)
-            total_ref[...] = total
-            basis_ref[...] = whole[...]
-            gather_end()
-            wide_ref[...] = wide_k[...]
+            basis_store.wait()
+            wide_store.wait()
 
         return carry
 
@@ -479,7 +484,7 @@
             jax.ShapeDtypeStruct((RANK, RANK), f32),
         ),
         in_specs=[pl.BlockSpec(memory_space=pl.ANY), vmem],
-        out_specs=(vmem, vmem, vmem, vmem),
+        out_specs=(pl.BlockSpec(memory_space=pl.ANY), pl.BlockSpec(memory_space=pl.ANY), vmem, vmem),
         scratch_shapes=[
             pltpu.VMEM((ROWS, PAD), bf16),
             pltpu.VMEM((PAD, RANK), bf16),
@@ -507,6 +512,7 @@
             pltpu.VMEM((RANK, RANK), f32),
             pltpu.VMEM((ROWS, RANK), f32),
             dma((4,)),
+            dma((2,)),
             dma((STEPS * 4, 3)),
             dma((STEPS * 4, 3)),
             dma((STEPS, 4)),
@@ -541,7 +547,6 @@
         at = pl.ds(i * 256, 256)
         loads.append(pltpu.make_async_copy(w_hbm.at[at, :], w_ref.at[at, :], w_sem.at[i]))
         loads[-1].start()
-    wide_load.wait()
 
     def prepare(t):
         at = pl.ds(pl.multiple_of(t * TILE, 128), TILE)
@@ -552,11 +557,16 @@
     scale = jnp.sqrt(jnp.sum(half * half, keepdims=True))
 
     def newton(i, pair):
+        return newton_step(pair, eye)
+
+    def newton_and_prepare(i, pair):
         prepare(i)
         return newton_step(pair, eye)
 
-    upper, inverse = lax.fori_loop(0, NS_ITERS, newton, (half / scale, eye))
-    prepare(NS_ITERS)
+    tiles = PAD // TILE
+    pair = lax.fori_loop(0, NS_ITERS - tiles, newton, (half / scale, eye))
+    wide_load.wait()
+    upper, inverse = lax.fori_loop(0, tiles, newton_and_prepare, pair)
     root = jnp.sqrt(scale)
     total = total_ref[...]
     quarter = mm(total.T, upper * root)
@@ -611,7 +621,7 @@
             pltpu.VMEM((ROWS, COLS), bf16),
             pltpu.VMEM((ROWS, RANK), f32),
             pltpu.VMEM((PAD, RANK), f32),
-            pltpu.VMEM((6 * RANK, COLS), bf16),
+            pltpu.VMEM((6 * RANK, PAD), bf16),
             pltpu.VMEM((ROWS, 3 * RANK), bf16),
             pltpu.VMEM((3 * RANK, COLS), bf16),
             pltpu.VMEM((ROWS, RANK), f32),

time: 223 us -> 221 us (level)
  no operation moved by 1% of the time
where the time goes in v5:
time: 221 us
  Pallas kernels  220 us (100%)
    pallas_call x1, Pallas kernels, factors(): pl.pallas_call(factors_kernel, name='factors', out_shape=(jax.ShapeDtypeS...  202 us
    pallas_call x1, Pallas kernels, residual(): pl.pallas_call(residual_kernel, name='residual', out_shape=(jax.ShapeDtyp...  18.1 us

profile of v5, /device:TPU:1, one launch (start us, length us, event | category | flops | bytes accessed | tf_op | source)
XLA Modules:
  0.0 221.0 jit_solution(7110025597354092460)
XLA Ops:
  0.6 202.1 %factors.1 = (f32[1024,128]{1,0:T(8,128)}, f32[5120,128]{1,0:T(8,128)}, f32[128,128]{1,0:T(8,128)}, f32[128,128]{1,0:T(8,128)}) custom-call(bf16[1024,4992]{1,0:T(8,128)(2,1)} %w_hbm.3, bf16[4992,128]{1,0:T(8,128)(2,1)} %sketch_ref.1), custom_call_target="tpu_custom_call" | custom-call | tf_op jit(solution)/shard_map/factors/pallas_call | solution.py:477
  202.7 18.1 %residual.1 = (f32[1024,128]{1,0:T(8,128)}, f32[128,4992]{1,0:T(8,128)}, bf16[1024,4992]{1,0:T(8,128)(2,1)}) custom-call(bf16[1024,4992]{1,0:T(8,128)(2,1)} %w_hbm.3, f32[1024,128]{1,0:T(8,128)} %get-tuple-element.7.basis_hbm, f32[5120,128]{1,0:T(8,128)} %get-tuple-element.8.wide_hbm, f32[128,128]{1,0:T(8,128)} %get-tuple-element.9.half_ref, ...), custom_call_target="tpu_custom_call" | custom-call | tf_op jit(solution)/shard_map/residual/pallas_call | solution.py:610
